TPU v7x, 256 devices: a whole 4x4x8 slice. The times are simulated.
256 devices in a mesh: dp: 128 (over x, y, z), group: 2 (over core).
Axes of the slice: x: 4, y: 4, z: 8, core: 2. Of those that a mesh axis runs over, the one named last changes fastest.
Arguments:
- tokens_in: bfloat16 [128, 256, 1536], P('dp', None, 'group'), may hold values from -24 to 24
- dw_kernel: float32 [7, 1536], P(None, 'group'), may hold values from -2 to 2
- point_weight: bfloat16 [1536, 1536], P(None, 'group'), may hold values from -0.15625 to 0.15625
- positive_emb: bfloat16 [128, 1536], P('dp', 'group'), may hold values from -0.15625 to 0.15625
- bank: bfloat16 [16384, 1536], P('dp', 'group'), may hold values from -0.15625 to 0.15625
- neg_owner: int32 [16384, 1], P('dp'), may hold values from 0 to 127; in each aligned block of 128 rows (0 to 127, 128 to 255, ...) at most 2 rows name the same one
- neg_block: int32 [16384], P('dp'), may hold values from 0 to 15
Outputs:
- grad_bank: float32 [16384, 1536], P('dp', 'group')
- grad_kernel: float32 [7, 1536], P(None, 'group')
- grad_weight: float32 [1536, 1536], P('dp', 'group')
Inputs may be any that keep to these rules, and one draw needn't show every extreme that they name: `neg_owner`: among the 128 requests of one batch shard (aligned blocks of 128 rows), no owner is named more than 2 times.
All inputs are finite; a program needn't handle non-finite values.
Results may differ from a plain program's by a relative error of at most 0.0036.
Values may be sent and summed in bfloat16 or wider, within the bound.
No kernel may reach another device: no remote copies, remote signals or barrier semaphores. Data moves between devices by JAX's collectives and lax.ppermute only.
A program may use at most 128 MiB of HBM per device.

v0:
```python
import jax
import jax.numpy as jnp
from jax import lax
from jax.sharding import PartitionSpec as P

ROWS = 8
CAP = 2


SOFTMAX_TEMPER = 0.07
LOSS_SCALE = 256.0
EPSILON = 1e-06
PRECISE = lax.Precision.HIGHEST


def depthwise(tokens, kernel):
    margin = kernel.shape[0] // 2
    seq_length = tokens.shape[1]
    padded = jnp.pad(tokens.astype(jnp.float32), ((0, 0), (margin, margin), (0, 0)))
    running_sum = jnp.zeros(tokens.shape, jnp.float32)
    for tap_index in range(kernel.shape[0]):
        running_sum = (
            running_sum + kernel[tap_index] * padded[:, tap_index : tap_index + seq_length, :]
        )
    return (running_sum, padded)


def kernel_term(grad_hidden, padded, tap_count):
    seq_length = grad_hidden.shape[1]
    return jnp.stack(
        [
            jnp.sum(grad_hidden * padded[:, tap_index : tap_index + seq_length, :], axis=(0, 1))
            for tap_index in range(tap_count)
        ]
    )


def gelu_back(mixed_out, cotangent):
    return jax.vjp(lambda entry_value: jax.nn.gelu(entry_value, approximate=True), mixed_out)[1](
        cotangent
    )[0]


def per_device(tokens_in, dw_kernel, point_weight, positive_emb, bank, neg_owner, neg_block):
    seq_count, seq_length, half_width = tokens_in.shape
    token_count = seq_count * seq_length
    device_count = lax.axis_size("dp")
    slot_count = device_count * CAP
    block_count = bank.shape[0] // ROWS
    request_count = neg_owner.shape[0]
    local_rows = bank.shape[0]
    local_end = seq_count + local_rows
    hidden_f, padded = depthwise(tokens_in, dw_kernel)
    hidden = hidden_f.astype(jnp.bfloat16).reshape(token_count, half_width)
    mixed_part = lax.dot_general(
        hidden, point_weight, (((1,), (1,)), ((), ())), preferred_element_type=jnp.float32
    )
    mixed_out = lax.psum_scatter(mixed_part, "group", scatter_dimension=1, tiled=True)
    activated = jax.nn.gelu(mixed_out, approximate=True)
    embedding = jnp.mean(
        tokens_in.astype(jnp.float32) + activated.reshape(seq_count, seq_length, half_width), axis=1
    )
    owners = neg_owner[:, 0]
    owner_hits = (owners[:, None] == jnp.arange(device_count, dtype=jnp.int32)[None, :]).astype(
        jnp.int32
    )
    earlier = jnp.cumsum(owner_hits, axis=0) - owner_hits
    rank_in_owner = jnp.sum(earlier * owner_hits, axis=1)
    slot_index = owners * CAP + rank_in_owner
    slot_hits = (slot_index[:, None] == jnp.arange(slot_count, dtype=jnp.int32)[None, :]).astype(
        jnp.int32
    )
    wanted = jnp.sum(slot_hits * (neg_block[:, None] + 1), axis=0) - 1
    asked_blocks = lax.all_to_all(
        wanted.reshape(device_count, CAP), "dp", split_axis=0, concat_axis=0, tiled=True
    )
    asked_flat = asked_blocks.reshape(slot_count)
    blocks_local = bank.reshape(block_count, ROWS, half_width)
    served = jnp.take(blocks_local, jnp.maximum(asked_flat, 0), axis=0)
    served = jnp.where((asked_flat >= 0)[:, None, None], served, jnp.zeros((), jnp.bfloat16))
    fetched = lax.all_to_all(
        served.reshape(device_count, CAP, ROWS, half_width),
        "dp",
        split_axis=0,
        concat_axis=0,
        tiled=True,
    )
    negatives = jnp.take(fetched.reshape(slot_count, ROWS, half_width), slot_index, axis=0).reshape(
        request_count * ROWS, half_width
    )
    key_rows = jnp.concatenate([positive_emb, bank, negatives], axis=0)
    column_count = key_rows.shape[0]
    key_float = key_rows.astype(jnp.float32)
    dots_part = lax.dot_general(embedding, key_float, (((1,), (1,)), ((), ())), precision=PRECISE)
    inner_products, embed_sq, key_sq = lax.psum(
        (dots_part, jnp.sum(embedding * embedding, axis=1), jnp.sum(key_float * key_float, axis=1)),
        "group",
    )
    embedding_norm = jnp.sqrt(embed_sq + EPSILON)
    key_length_norm = jnp.sqrt(key_sq + EPSILON)
    score_matrix = inner_products / (
        SOFTMAX_TEMPER * embedding_norm[:, None] * key_length_norm[None, :]
    )
    exponent = jnp.exp(score_matrix)
    weights = exponent / jnp.sum(exponent, axis=1, keepdims=True)
    score_gradient = LOSS_SCALE * (weights - jnp.eye(seq_count, column_count, dtype=jnp.float32))
    blend_factor = score_gradient / (SOFTMAX_TEMPER * key_length_norm[None, :])
    unit_query = embedding / embedding_norm[:, None]
    row_weight = jnp.sum(score_gradient * score_matrix, axis=1)
    column_weight = jnp.sum(score_gradient * score_matrix, axis=0)
    key_scale = column_weight / (key_length_norm * key_length_norm)
    query_dir = jnp.dot(blend_factor, key_float, precision=PRECISE)
    embed_grad = (query_dir - row_weight[:, None] * unit_query) / embedding_norm[:, None]
    key_grad = (
        lax.dot_general(blend_factor, unit_query, (((0,), (0,)), ((), ())), precision=PRECISE)
        - key_scale[:, None] * key_float
    )
    local_grad = key_grad[seq_count:local_end]
    neg_grad = key_grad[local_end:].reshape(request_count, ROWS, half_width)
    outgoing = jnp.zeros((slot_count, ROWS, half_width), jnp.float32).at[slot_index].set(neg_grad)
    returned = lax.all_to_all(
        outgoing.reshape(device_count, CAP, ROWS, half_width),
        "dp",
        split_axis=0,
        concat_axis=0,
        tiled=True,
    )
    block_pick = (asked_flat[:, None] == jnp.arange(block_count, dtype=jnp.int32)[None, :]).astype(
        jnp.float32
    )
    remote = lax.dot_general(
        block_pick,
        returned.reshape(slot_count, ROWS * half_width),
        (((0,), (0,)), ((), ())),
        precision=PRECISE,
    )
    bank_grad = local_grad + remote.reshape(local_rows, half_width)
    act_grad = jnp.broadcast_to(
        (embed_grad / seq_length)[:, None, :], (seq_count, seq_length, half_width)
    ).reshape(token_count, half_width)
    mixed_grad = gelu_back(mixed_out, act_grad).astype(jnp.bfloat16)
    mixed_all = lax.all_gather(mixed_grad, "group", axis=1, tiled=True)
    hidden_grad = jnp.dot(mixed_all, point_weight, preferred_element_type=jnp.float32)
    kernel_part = kernel_term(
        hidden_grad.reshape(seq_count, seq_length, half_width), padded, dw_kernel.shape[0]
    )
    kernel_grad = lax.psum(kernel_part, "dp") / device_count
    weight_grad = (
        lax.psum_scatter(
            lax.dot_general(
                mixed_all, hidden, (((0,), (0,)), ((), ())), preferred_element_type=jnp.float32
            ),
            "dp",
            scatter_dimension=0,
            tiled=True,
        )
        / device_count
    )
    return (bank_grad, kernel_grad, weight_grad)


def solution(mesh):
    in_specs = (
        P("dp", None, "group"),
        P(None, "group"),
        P(None, "group"),
        P("dp", "group"),
        P("dp", "group"),
        P("dp", None),
        P("dp"),
    )
    out_specs = (P("dp", "group"), P(None, "group"), P("dp", "group"))
    return jax.shard_map(
        per_device, mesh=mesh, in_specs=in_specs, out_specs=out_specs, check_vma=False
    )
```

profile of v0, /device:TPU:8, one launch (start us, length us, event | category | flops | bytes accessed | tf_op | source)
XLA Modules:
  0.0 1545.0 jit_solution(61074231811996590)
XLA Ops:
  10.7 26.2 %all_to_all.16 = s32[128,1,2]{2,1,0:T(1,128)S(1)} all-to-all(s32[128,1,2]{2,1,0:T(1,128)S(1)} %bitcast.66), channel_id=1, replica_groups=mesh['dp'=128,'group'=2] {'dp'}, dimensions={0} | all-to-all | bytes 2048 | tf_op jit(solution)/shard_map/all_to_all | solution.py:74
  44.4 7.9 all-to-all-start.1
  56.2 15.8 %reduce-scatter.4.cloned.1.call-done = f32[256,768]{1,0:T(8,128)} async-done(((f32[256,1536]{1,0:T(8,128)}), f32[256,768]{1,0:T(8,128)}) %reduce-scatter.4.cloned.1.call-update) | async-done | bytes 786448 | tf_op jit(solution)/shard_map/reduce_scatter | solution.py:58
  74.0 51.0 %all-to-all-done.1 = bf16[128,2,8,768]{3,2,1,0:T(8,128)(2,1)} async-done(((bf16[128,2,8,768]{3,2,1,0:T(8,128)(2,1)}), bf16[128,2,8,768]{3,2,1,0:T(8,128)(2,1)}, u32[]{:S(2)}, u32[]{:S(2)}) %all-to-all-start.1) | async-done | bytes 3145760 | tf_op jit(solution)/shard_map/all_to_all | solution.py:81
  125.0 3.7 gather_fusion.1
  131.5 10.8 concatenate.3
  147.3 4.5 all-reduce.3
  164.7 18.4 %scatter_fusion = f32[256,8,768]{2,1,0:T(8,128)} fusion(f32[256,8,768]{2,1,0:T(8,128)} %broadcast_in_dim.66, s32[128]{0:T(128)S(1)} %get-tuple-element.37, f32[128,8,768]{2,1,0:T(8,128)} %slice_bitcast_fusion), kind=kCustom, calls=%fused_computation.2 | custom fusion | bytes 9437696 | tf_op jit(solution)/shard_map/scatter | solution.py:120
  183.1 10.3 all-to-all-start.2
  199.3 485.4 %fusion = f32[16,768]{1,0:T(8,128)} fusion(f32[1536,768]{1,0:T(8,128)} %fusion.12), kind=kCustom, calls=%all-reduce-scatter | all-reduce-scatter fusion | flops 1572865 | bytes 4768768
  692.4 29.6 %collective-permute-start.27 = (f32[16,768]{1,0:T(8,128)}, f32[16,768]{1,0:T(8,128)}, u32[]{:S(2)}, u32[]{:S(2)}) collective-permute-start(f32[16,768]{1,0:T(8,128)} %fusion), channel_id=1, source_target_pairs={{0,56},{2,58},{4,60},{6,62},{8,64},{10,66},{12,68},{14,70},{16,72}... | collective-permute-start | bytes 147464
  734.0 3.7 collective-permute-start.20
  737.7 5.4 collective-permute-start.19
  743.1 4.6 collective-permute-start.18
  749.7 3.5 collective-permute-start.16
  759.2 4.3 collective-permute-start.12
  763.6 3.8 collective-permute-start.11
  767.4 4.0 collective-permute-start.10
  779.4 4.0 collective-permute-start.8
  790.7 4.3 multiply_reduce_fusion
  795.1 664.8 %psum.31 = f32[7,768]{1,0:T(8,128)S(1)} all-reduce(f32[7,768]{1,0:T(8,128)S(1)} %stack.31), channel_id=1, replica_groups=mesh['dp'=128,'group'=2] {'dp'}, use_global_device_ids=true, to_apply=%region_20.21 | all-reduce | flops 5376 | bytes 43008 | tf_op jit(solution)/shard_map/psum | solution.py:147
  1470.5 4.7 collective-permute-done.4
  1478.7 48.4 %concatenate.4 = f32[524,768]{1,0:T(8,128)} concatenate(f32[12,768]{1,0:T(8,128)} %copy-done.9, f32[16,768]{1,0:T(8,128)} %collective-permute-done.30, f32[16,768]{1,0:T(8,128)} %collective-permute-done.29, f32[16,768]{1,0:T(8,128)} %collective-permute-done.28, f32[16,768]{1,0:T(8,128)} %collective-permute-done.27, f32[16,768]{1,0:T(8,128)} %collective-permute-done.26, ...), dimensions={0} | concatenate | bytes 3219456
  1528.7 5.4 copy.27
  (148 shorter events, 104.3 us)
Async XLA Ops:
  44.4 80.7 %all-to-all-start.1 = ((bf16[128,2,8,768]{3,2,1,0:T(8,128)(2,1)}), bf16[128,2,8,768]{3,2,1,0:T(8,128)(2,1)}, u32[]{:S(2)}, u32[]{:S(2)}) async-start(bf16[128,2,8,768]{3,2,1,0:T(8,128)(2,1)} %select_select_fusion), calls=%async_computation.2 | async-start | bytes 6291456 | tf_op jit(solution)/shard_map/all_to_all | solution.py:81
  52.3 19.7 %reduce-scatter.4.cloned.1.call-start = ((), (), s32[]{:S(2)}) async-start(), calls=%async_computation.4 | async-start | bytes 2359296 | tf_op jit(solution)/shard_map/reduce_scatter | solution.py:58
  183.1 1345.6 %all-to-all-start.2 = ((f32[128,2,8,768]{3,2,1,0:T(8,128)}), f32[128,2,8,768]{3,2,1,0:T(8,128)}, u32[]{:S(2)}, u32[]{:S(2)}) async-start(f32[128,2,8,768]{3,2,1,0:T(8,128)} %bitcast.63), calls=%async_computation.3 | async-start | bytes 12582912 | tf_op jit(solution)/shard_map/all_to_all | solution.py:121
  684.6 39.9 %collective-permute-start.30 = (f32[16,768]{1,0:T(8,128)}, f32[16,768]{1,0:T(8,128)}, u32[]{:S(2)}, u32[]{:S(2)}) collective-permute-start(f32[16,768]{1,0:T(8,128)} %fusion), channel_id=1, source_target_pairs={{0,62},{2,64},{4,66},{6,68},{8,70},{10,72},{12,74},{14,76},{16,78}... | collective-permute-start | bytes 147464
  687.3 34.7 %collective-permute-start.31 = (f32[12,768]{1,0:T(8,128)S(1)}, f32[12,768]{1,0:T(8,128)S(1)}, u32[]{:S(2)}, u32[]{:S(2)}) collective-permute-start(f32[12,768]{1,0:T(8,128)S(1)} %slice.74), channel_id=1, source_target_pairs={{0,64},{2,66},{4,68},{6,70},{8,72},{10,74},{12,76},{14,78},{16,80}... | collective-permute-start | bytes 110600
  688.6 37.8 %collective-permute-start.29 = (f32[16,768]{1,0:T(8,128)}, f32[16,768]{1,0:T(8,128)}, u32[]{:S(2)}, u32[]{:S(2)}) collective-permute-start(f32[16,768]{1,0:T(8,128)} %fusion), channel_id=1, source_target_pairs={{0,60},{2,62},{4,64},{6,66},{8,68},{10,70},{12,72},{14,74},{16,76}... | collective-permute-start | bytes 147464
  690.5 37.8 %collective-permute-start.28 = (f32[16,768]{1,0:T(8,128)}, f32[16,768]{1,0:T(8,128)}, u32[]{:S(2)}, u32[]{:S(2)}) collective-permute-start(f32[16,768]{1,0:T(8,128)} %fusion), channel_id=1, source_target_pairs={{0,58},{2,60},{4,62},{6,64},{8,66},{10,68},{12,70},{14,72},{16,74}... | collective-permute-start | bytes 147464
  692.4 37.8 %collective-permute-start.27 = (f32[16,768]{1,0:T(8,128)}, f32[16,768]{1,0:T(8,128)}, u32[]{:S(2)}, u32[]{:S(2)}) collective-permute-start(f32[16,768]{1,0:T(8,128)} %fusion), channel_id=1, source_target_pairs={{0,56},{2,58},{4,60},{6,62},{8,64},{10,66},{12,68},{14,70},{16,72}... | collective-permute-start | bytes 147464
  730.2 17.5 %collective-permute-start.22 = (f32[16,768]{1,0:T(8,128)}, f32[16,768]{1,0:T(8,128)}, u32[]{:S(2)}, u32[]{:S(2)}) collective-permute-start(f32[16,768]{1,0:T(8,128)} %fusion), channel_id=1, source_target_pairs={{0,46},{2,48},{4,50},{6,52},{8,54},{10,56},{12,58},{14,60},{16,62}... | collective-permute-start | bytes 147464
  732.1 17.5 %collective-permute-start.21 = (f32[16,768]{1,0:T(8,128)}, f32[16,768]{1,0:T(8,128)}, u32[]{:S(2)}, u32[]{:S(2)}) collective-permute-start(f32[16,768]{1,0:T(8,128)} %fusion), channel_id=1, source_target_pairs={{0,44},{2,46},{4,48},{6,50},{8,52},{10,54},{12,56},{14,58},{16,60}... | collective-permute-start | bytes 147464
  734.0 19.2 %collective-permute-start.20 = (f32[16,768]{1,0:T(8,128)}, f32[16,768]{1,0:T(8,128)}, u32[]{:S(2)}, u32[]{:S(2)}) collective-permute-start(f32[16,768]{1,0:T(8,128)} %fusion), channel_id=1, source_target_pairs={{0,42},{2,44},{4,46},{6,48},{8,50},{10,52},{12,54},{14,56},{16,58}... | collective-permute-start | bytes 147464
  737.7 17.4 %collective-permute-start.19 = (f32[16,768]{1,0:T(8,128)}, f32[16,768]{1,0:T(8,128)}, u32[]{:S(2)}, u32[]{:S(2)}) collective-permute-start(f32[16,768]{1,0:T(8,128)} %fusion), channel_id=1, source_target_pairs={{0,40},{2,42},{4,44},{6,46},{8,48},{10,50},{12,52},{14,54},{16,56}... | collective-permute-start | bytes 147464
  755.1 21.3 %collective-permute-start.14 = (f32[16,768]{1,0:T(8,128)}, f32[16,768]{1,0:T(8,128)}, u32[]{:S(2)}, u32[]{:S(2)}) collective-permute-start(f32[16,768]{1,0:T(8,128)} %fusion), channel_id=1, source_target_pairs={{0,30},{2,32},{4,34},{6,36},{8,38},{10,40},{12,42},{14,44},{16,46}... | collective-permute-start | bytes 147464
  757.2 22.2 %collective-permute-start.13 = (f32[16,768]{1,0:T(8,128)}, f32[16,768]{1,0:T(8,128)}, u32[]{:S(2)}, u32[]{:S(2)}) collective-permute-start(f32[16,768]{1,0:T(8,128)} %fusion), channel_id=1, source_target_pairs={{0,28},{2,30},{4,32},{6,34},{8,36},{10,38},{12,40},{14,42},{16,44}... | collective-permute-start | bytes 147464
  759.2 24.2 %collective-permute-start.12 = (f32[16,768]{1,0:T(8,128)}, f32[16,768]{1,0:T(8,128)}, u32[]{:S(2)}, u32[]{:S(2)}) collective-permute-start(f32[16,768]{1,0:T(8,128)} %fusion), channel_id=1, source_target_pairs={{0,26},{2,28},{4,30},{6,32},{8,34},{10,36},{12,38},{14,40},{16,42}... | collective-permute-start | bytes 147464
  763.6 21.7 %collective-permute-start.11 = (f32[16,768]{1,0:T(8,128)}, f32[16,768]{1,0:T(8,128)}, u32[]{:S(2)}, u32[]{:S(2)}) collective-permute-start(f32[16,768]{1,0:T(8,128)} %fusion), channel_id=1, source_target_pairs={{0,24},{2,26},{4,28},{6,30},{8,32},{10,34},{12,36},{14,38},{16,40}... | collective-permute-start | bytes 147464
  767.4 20.8 %collective-permute-start.10 = (f32[16,768]{1,0:T(8,128)}, f32[16,768]{1,0:T(8,128)}, u32[]{:S(2)}, u32[]{:S(2)}) collective-permute-start(f32[16,768]{1,0:T(8,128)} %fusion), channel_id=1, source_target_pairs={{0,22},{2,24},{4,26},{6,28},{8,30},{10,32},{12,34},{14,36},{16,38}... | collective-permute-start | bytes 147464
  776.4 683.6 %collective-permute-start.9 = (f32[16,768]{1,0:T(8,128)}, f32[16,768]{1,0:T(8,128)}, u32[]{:S(2)}, u32[]{:S(2)}) collective-permute-start(f32[16,768]{1,0:T(8,128)} %fusion), channel_id=1, source_target_pairs={{0,20},{2,22},{4,24},{6,26},{8,28},{10,30},{12,32},{14,34},{16,36}... | collective-permute-start | bytes 147464
  779.4 682.5 %collective-permute-start.8 = (f32[16,768]{1,0:T(8,128)}, f32[16,768]{1,0:T(8,128)}, u32[]{:S(2)}, u32[]{:S(2)}) collective-permute-start(f32[16,768]{1,0:T(8,128)} %fusion), channel_id=1, source_target_pairs={{0,18},{2,20},{4,22},{6,24},{8,26},{10,28},{12,30},{14,32},{16,34}... | collective-permute-start | bytes 147464
  783.4 680.4 %collective-permute-start.7 = (f32[16,768]{1,0:T(8,128)}, f32[16,768]{1,0:T(8,128)}, u32[]{:S(2)}, u32[]{:S(2)}) collective-permute-start(f32[16,768]{1,0:T(8,128)} %fusion), channel_id=1, source_target_pairs={{0,16},{2,18},{4,20},{6,22},{8,24},{10,26},{12,28},{14,30},{16,32}... | collective-permute-start | bytes 147464
  785.3 680.4 %collective-permute-start.6 = (f32[16,768]{1,0:T(8,128)}, f32[16,768]{1,0:T(8,128)}, u32[]{:S(2)}, u32[]{:S(2)}) collective-permute-start(f32[16,768]{1,0:T(8,128)} %fusion), channel_id=1, source_target_pairs={{0,14},{2,16},{4,18},{6,20},{8,22},{10,24},{12,26},{14,28},{16,30}... | collective-permute-start | bytes 147464
  788.1 679.6 %collective-permute-start.5 = (f32[16,768]{1,0:T(8,128)}, f32[16,768]{1,0:T(8,128)}, u32[]{:S(2)}, u32[]{:S(2)}) collective-permute-start(f32[16,768]{1,0:T(8,128)} %fusion), channel_id=1, source_target_pairs={{0,12},{2,14},{4,16},{6,18},{8,20},{10,22},{12,24},{14,26},{16,28}... | collective-permute-start | bytes 147464
  1460.0 15.2 collective-permute-start.4
  1461.9 16.8 %collective-permute-start.3 = (f32[16,768]{1,0:T(8,128)}, f32[16,768]{1,0:T(8,128)S(1)}, u32[]{:S(2)}, u32[]{:S(2)}) collective-permute-start(f32[16,768]{1,0:T(8,128)} %fusion), channel_id=1, source_target_pairs={{0,8},{2,10},{4,12},{6,14},{8,16},{10,18},{12,20},{14,22},{16,24},... | collective-permute-start | bytes 147464
  (25 other events, 1402.3 us)
Sparse Core Ops, SparseCore 0:
  56.1 15.8 reduce-scatter.3
where the time goes:
time: 1570 us; the launch traced here: 1540 us
  blocking collectives  1180 us (75%)
  starting transfers between devices  128 us (8%)
  local copies, waits for them, and re-layouts  102 us (6%)
  waiting for transfers between devices  75.1 us (5%)
  other arithmetic  24.1 us (2%)
  matrix products  16.6 us (1%)
  between operations  16 us (1%)
    psum x1, blocking collectives, per_device(): kernel_grad = lax.psum(kernel_part, 'dp') / device_count  665 us
    unnamed x1, blocking collectives  485 us
    unnamed x32, starting transfers between devices  109 us
    unnamed x32, local copies, waits for them, and re-layouts  58.4 us
    all_to_all x1, waiting for transfers between devices, per_device(): lax.all_to_all(served.reshape(device_count, CAP, ROWS, half_width), 'dp',...  51 us
  transfers between devices with their start and end apart: 35, of which 4 were waited for; matrix products, arithmetic and copies ran while one was open for 36% of the time, Pallas kernels for 0%

commit v1 on v0

v1 whole, which is shorter than its diff:
```python
import jax
import jax.numpy as jnp
from jax import lax
from jax.experimental import pallas as pl
from jax.experimental.pallas import tpu as pltpu
from jax.sharding import Mesh, PartitionSpec as P

KW = 7
LEN = 256
HALF = 768
N_DP = 128
NX, NY, NZ = 4, 4, 8
PLANE = NX * NY
ROWS = 8
OWN = 128
OUT_ROWS = 12
Z_ROWS = OUT_ROWS * NZ
PACK = 16
EXTRA = 128
WIDE = HALF + EXTRA
LANES = 128
COLS = HALF // LANES

TEMPER = 0.07
SCALE = 256.0
EPSILON = 1e-06
GELU_C = 0.7978845608028654
GELU_A = 0.044715
PRECISE = lax.Precision.HIGHEST
F32 = jnp.float32
BF16 = jnp.bfloat16

DP = ("x", "y", "z")
SWAP = [(0, 1), (1, 0)]
VMEM_BYTES = 50 * 2**20

NT = (((1,), (1,)), ((), ()))
NN = (((1,), (0,)), ((), ()))
TN = (((0,), (0,)), ((), ()))


def dot(a, b, dims, precision=None):
    return lax.dot_general(a, b, dims, precision=precision, preferred_element_type=F32)


def call(body, outs, name, scratch=(), scalars=0, n_in=0, flops=0):
    smem = [pl.BlockSpec(memory_space=pltpu.SMEM)] * scalars
    vmem = [pl.BlockSpec(memory_space=pltpu.VMEM)] * n_in
    return pl.pallas_call(
        body,
        out_shape=[jax.ShapeDtypeStruct(s, d) for s, d in outs],
        in_specs=smem + vmem,
        out_specs=[pl.BlockSpec(memory_space=pltpu.VMEM)] * len(outs),
        scratch_shapes=list(scratch),
        compiler_params=pltpu.CompilerParams(vmem_limit_bytes=VMEM_BYTES),
        cost_estimate=pl.CostEstimate(flops=flops, bytes_accessed=1 << 20, transcendentals=0),
        name=name,
    )


def fill_padded(tokens_ref, pad):
    pad[0:8, :] = jnp.zeros((8, HALF), F32)
    pad[LEN + 8 : LEN + 16, :] = jnp.zeros((8, HALF), F32)
    for t in range(0, LEN, 32):
        pad[8 + t : 40 + t, :] = tokens_ref[t : t + 32, :].astype(F32)


def conv_body(place, tokens_ref, dw_ref, w_ref, hidden_ref, other_ref, pad):
    fill_padded(tokens_ref, pad)
    for t in range(0, LEN, 32):
        total = jnp.zeros((32, HALF), F32)
        for k in range(KW):
            total = total + dw_ref[k : k + 1, :] * pad[5 + k + t : 37 + k + t, :]
        hidden_ref[t : t + 32, :] = total.astype(BF16)
    start = pl.multiple_of((1 - place[0]) * HALF, HALF)
    other_ref[...] = dot(hidden_ref[...], w_ref[pl.ds(start, HALF), :], NT)


def own_body(place, hidden_ref, w_ref, owner_ref, block_ref, own_ref, table_ref):
    start = pl.multiple_of(place[0] * HALF, HALF)
    own_ref[...] = dot(hidden_ref[...], w_ref[pl.ds(start, HALF), :], NT)
    lane = lax.broadcasted_iota(jnp.int32, (OWN, LANES), 1)
    named = (owner_ref[...] == lane).astype(F32)
    blocks = jnp.broadcast_to(block_ref[...].astype(F32), (LANES, OWN)).T
    wanted = (blocks == lane.astype(F32)).astype(F32)
    table_ref[...] = dot(named.T.astype(BF16), wanted.astype(BF16), NN)


def embed_body(own_ref, other_ref, tokens_ref, table_ref, slope_ref, emb_ref, send_ref):
    total = jnp.zeros((8, HALF), F32)
    for t in range(0, LEN, 32):
        x = own_ref[t : t + 32, :] + other_ref[t : t + 32, :]
        sq = x * x
        th = jnp.tanh(GELU_C * x * (1.0 + GELU_A * sq))
        half = 0.5 * (1.0 + th)
        slope_ref[t : t + 32, :] = half + (0.5 * GELU_C) * x * (1.0 - th * th) * (
            1.0 + (3.0 * GELU_A) * sq
        )
        y = tokens_ref[t : t + 32, :].astype(F32) + x * half
        total = total + (y[0:8] + y[8:16]) + (y[16:24] + y[24:32])
    emb = jnp.sum(total, axis=0, keepdims=True) * (1.0 / LEN)
    emb_ref[...] = jnp.broadcast_to(emb, (8, HALF))
    send_ref[:, 0, 0:HALF] = jnp.broadcast_to(emb, (N_DP, HALF))
    send_ref[:, 0, HALF:WIDE] = table_ref[...]


def dots_body(recv_ref, bank_ref, emb_ref, pos_ref, packet_ref):
    e = recv_ref[:, 0, 0:HALF]
    key = bank_ref[...].astype(F32)
    packet_ref[0:OWN, :] = dot(key, e, NT, PRECISE)
    ones = jnp.ones((8, HALF), F32)
    packet_ref[OWN : OWN + 8, :] = dot(ones, e * e, NT, PRECISE)
    ksq = jnp.sum(key * key, axis=1, keepdims=True)
    packet_ref[OWN + 8 : 2 * OWN + 8, :] = jnp.broadcast_to(ksq, (OWN, LANES))
    emb = emb_ref[0:1, :]
    pos = pos_ref[...].astype(F32)
    rows = (emb * emb, emb * pos, pos * pos)
    for i in range(3):
        value = jnp.sum(rows[i], axis=1, keepdims=True)
        packet_ref[2 * OWN + 8 + 8 * i : 2 * OWN + 16 + 8 * i, :] = jnp.broadcast_to(
            value, (8, LANES)
        )


PACKET = 2 * OWN + 32


def scores_body(
    place, mine_ref, theirs_ref, recv_ref, bank_ref, send_ref, coef_ref, kcoef_ref, scal_ref
):
    full = mine_ref[...] + theirs_ref[...]
    en = jnp.sqrt(full[OWN : OWN + 1] + EPSILON)
    kn = jnp.sqrt(full[OWN + 8 : 2 * OWN + 8] + EPSILON)
    scal_ref[...] = full[2 * OWN + 8 : PACKET]
    score = full[0:OWN] / (TEMPER * en * kn)
    count = recv_ref[:, 0, HALF:WIDE].T
    row = lax.broadcasted_iota(jnp.int32, (OWN, LANES), 0)
    lane = lax.broadcasted_iota(jnp.int32, (OWN, LANES), 1)
    spread = (row // ROWS == lane).astype(F32)
    count = dot(spread.astype(BF16), count.astype(BF16), NN)
    count = count + (lane == place[1]).astype(F32)
    ec = count * jnp.exp(score)
    z = jnp.sum(ec, axis=0, keepdims=True)
    s = jnp.sum(ec * score, axis=0, keepdims=True)
    blend = ec / kn
    coef_ref[...] = (SCALE / TEMPER) * blend / en
    kcoef_ref[...] = SCALE * ec * score / (kn * kn)
    send_ref[:, 0, 0:HALF] = dot(blend.T, bank_ref[...].astype(F32), NN, PRECISE)
    zs = jnp.where(row == 0, jnp.broadcast_to(z, (OWN, LANES)), jnp.broadcast_to(s, (OWN, LANES)))
    send_ref[:, 0, HALF:WIDE] = zs.T


def grad_body(place, recv_ref, emb_ref, pos_ref, scal_ref, slope_ref, mixed_ref, z_ref):
    total = jnp.sum(recv_ref[:, 0, :], axis=0, keepdims=True)
    esq = scal_ref[0:1, 0:1]
    inner = scal_ref[8:9, 0:1]
    psq = scal_ref[16:17, 0:1]
    en = jnp.sqrt(esq + EPSILON)
    pn = jnp.sqrt(psq + EPSILON)
    score = inner / (TEMPER * en * pn)
    hit = jnp.exp(score)
    z = total[:, HALF : HALF + 1] + hit
    s = total[:, HALF + 1 : HALF + 2] + hit * score
    row_weight = SCALE * (s / z - score)
    unit = emb_ref[0:1, :] / en
    pos = pos_ref[...].astype(F32)
    direction = (SCALE / TEMPER) * (total[:, 0:HALF] / z + ((hit / z - 1.0) / pn) * pos)
    grad = (direction - row_weight * unit) / en * (1.0 / LEN)
    for t in range(0, LEN, 32):
        mixed_ref[t : t + 32, :] = (slope_ref[t : t + 32, :] * grad).astype(BF16)
    lane = lax.broadcasted_iota(jnp.int32, (8, HALF), 1)
    z_ref[...] = jnp.where(lane == place[1], jnp.broadcast_to(z, (8, HALF)), 0.0)


def weight_body(
    place, mine_ref, theirs_ref, hidden_ref, w_ref, tokens_ref, z_ref, send_ref, pad, small
):
    fill_padded(tokens_ref, pad)
    g = place[0]
    first = pl.multiple_of(g * HALF, HALF)
    second = pl.multiple_of((1 - g) * HALF, HALF)
    hidden_grad = dot(mine_ref[...], w_ref[pl.ds(first, HALF), :], NN)
    hidden_grad = hidden_grad + dot(theirs_ref[...], w_ref[pl.ds(second, HALF), :], NN)
    for k in range(KW):
        small[k : k + 1, :] = jnp.sum(
            hidden_grad * pad[5 + k : 5 + k + LEN, :], axis=0, keepdims=True
        )
    small[KW : KW + 1, :] = z_ref[0:1, :]
    value = small[...]
    upper = value.astype(BF16).astype(F32)
    packed = jnp.concatenate([upper, value - upper], axis=0).astype(BF16)
    for p in range(PLANE):
        send_ref[p, Z_ROWS : Z_ROWS + PACK, :] = packed
    per = PLANE // 2
    mine = dot(mine_ref[...], hidden_ref[...], TN).astype(BF16)
    theirs = dot(theirs_ref[...], hidden_ref[...], TN).astype(BF16)
    for p in range(per):
        send_ref[g * per + p, 0:Z_ROWS, :] = mine[p * Z_ROWS : (p + 1) * Z_ROWS, :]
        send_ref[(1 - g) * per + p, 0:Z_ROWS, :] = theirs[p * Z_ROWS : (p + 1) * Z_ROWS, :]


BLOCK = OUT_ROWS + 8


def plane_body(recv_ref, send_ref, total):
    for r in range(0, Z_ROWS + PACK, 16):
        acc = recv_ref[0, r : r + 16, :].astype(F32)
        for p in range(1, PLANE):
            acc = acc + recv_ref[p, r : r + 16, :].astype(F32)
        total[r : r + 16, :] = acc
    rest = total[Z_ROWS : Z_ROWS + 8, :] + total[Z_ROWS + 8 : Z_ROWS + 16, :]
    for c in range(COLS):
        cols = slice(c * LANES, (c + 1) * LANES)
        for z in range(NZ):
            send_ref[z, c * BLOCK : c * BLOCK + OUT_ROWS, :] = total[
                z * OUT_ROWS : (z + 1) * OUT_ROWS, cols
            ]
            send_ref[z, c * BLOCK + OUT_ROWS : (c + 1) * BLOCK, :] = rest[:, cols]


def final_body(
    recv_ref, coef_ref, kcoef_ref, first_ref, bank_ref, bank_out, kernel_out, weight_out, total
):
    acc = recv_ref[0]
    for z in range(1, NZ):
        acc = acc + recv_ref[z]
    total[...] = acc
    for c in range(COLS):
        cols = slice(c * LANES, (c + 1) * LANES)
        base = c * BLOCK
        weight_out[:, cols] = total[base : base + OUT_ROWS, :] * (1.0 / N_DP)
        kernel_out[:, cols] = total[base + OUT_ROWS : base + OUT_ROWS + KW, :] * (1.0 / N_DP)
    inverse = 1.0 / total[BLOCK - 1 : BLOCK, :]
    coef = coef_ref[...] * inverse
    scale = jnp.sum(kcoef_ref[...] * inverse, axis=1, keepdims=True)
    product = dot(coef, first_ref[:, 0, 0:HALF], NN, PRECISE)
    bank_out[...] = product - scale * bank_ref[...].astype(F32)


def exchange(value, axes):
    return lax.all_to_all(value, axes, split_axis=0, concat_axis=0, tiled=True)


def per_device(tokens_in, dw_kernel, point_weight, positive_emb, bank, neg_owner, neg_block):
    tokens = tokens_in.reshape(LEN, HALF)
    g = lax.axis_index("group")
    d = (lax.axis_index("x") * NY + lax.axis_index("y")) * NZ + lax.axis_index("z")
    place = jnp.stack([g, d]).astype(jnp.int32)
    pad = pltpu.VMEM((LEN + 16, HALF), F32)
    flops = 2 * LEN * HALF * HALF

    hidden, other = call(
        conv_body,
        [((LEN, HALF), BF16), ((LEN, HALF), F32)],
        "conv_and_other_half",
        [pad],
        scalars=1,
        n_in=3,
        flops=flops,
    )(place, tokens, dw_kernel, point_weight)
    theirs = lax.ppermute(other, "group", SWAP)
    own, table = call(
        own_body,
        [((LEN, HALF), F32), ((N_DP, EXTRA), F32)],
        "own_half_and_requests",
        scalars=1,
        n_in=4,
        flops=flops,
    )(place, hidden, point_weight, neg_owner, neg_block.reshape(1, OWN))
    slope, emb, send = call(
        embed_body,
        [((LEN, HALF), F32), ((8, HALF), F32), ((N_DP, 1, WIDE), F32)],
        "embedding",
        n_in=4,
    )(own, theirs, tokens, table)
    gathered = exchange(send, DP)
    (packet,) = call(dots_body, [((PACKET, LANES), F32)], "inner_products", n_in=4)(
        gathered, bank, emb, positive_emb
    )
    packet_theirs = lax.ppermute(packet, "group", SWAP)
    send, coef, kcoef, scal = call(
        scores_body,
        [
            ((N_DP, 1, WIDE), F32),
            ((OWN, LANES), F32),
            ((OWN, LANES), F32),
            ((24, LANES), F32),
        ],
        "scores",
        scalars=1,
        n_in=4,
    )(place, packet, packet_theirs, gathered, bank)
    sums = exchange(send, DP)
    mixed, z = call(
        grad_body,
        [((LEN, HALF), BF16), ((8, HALF), F32)],
        "mixed_gradient",
        scalars=1,
        n_in=5,
    )(place, sums, emb, positive_emb, scal, slope)
    mixed_theirs = lax.ppermute(mixed, "group", SWAP)
    (send,) = call(
        weight_body,
        [((PLANE, Z_ROWS + PACK, HALF), BF16)],
        "weight_gradient",
        [pad, pltpu.VMEM((8, HALF), F32)],
        scalars=1,
        n_in=6,
    )(place, mixed, mixed_theirs, hidden, point_weight, tokens, z)
    planes = exchange(send, ("x", "y"))
    (send,) = call(
        plane_body,
        [((NZ, COLS * BLOCK, LANES), F32)],
        "sum_over_plane",
        [pltpu.VMEM((Z_ROWS + PACK, HALF), F32)],
        n_in=1,
    )(planes)
    lines = exchange(send, "z")
    return tuple(
        call(
            final_body,
            [((OWN, HALF), F32), ((KW, HALF), F32), ((OUT_ROWS, HALF), F32)],
            "outputs",
            [pltpu.VMEM((COLS * BLOCK, LANES), F32)],
            n_in=5,
        )(lines, coef, kcoef, gathered, bank)
    )


def solution(mesh):
    factored = Mesh(mesh.devices.reshape(NX, NY, NZ, 2), ("x", "y", "z", "group"))
    in_specs = (
        P(DP, None, "group"),
        P(None, "group"),
        P(None, "group"),
        P(DP, "group"),
        P(DP, "group"),
        P(DP, None),
        P(DP),
    )
    out_specs = (P(DP, "group"), P(None, "group"), P(DP, "group"))
    return jax.shard_map(
        per_device, mesh=factored, in_specs=in_specs, out_specs=out_specs, check_vma=False
    )
```

time: 1570 us -> 141 us (0.09); the launches traced: 1540 us -> 141 us
  blocking collectives: 1180 us -> 118 us
  starting transfers between devices: 128 us -> 0.19 us
  local copies, waits for them, and re-layouts: 102 us -> 3.54 us
  waiting for transfers between devices: 75.1 us -> 4.46 us
  other arithmetic: 24.1 us -> 0.08 us
  matrix products: 16.6 us -> 0 us
    psum x2 -> x0, blocking collectives: 669 us -> none  [the longest x1 665 us: per_device(): kernel_grad = lax.psum(kernel_part, 'dp') / device_count]
    unnamed x1 -> x0, blocking collectives: 485 us -> none
    unnamed x32 -> x0, starting transfers between devices: 109 us -> none
    all_to_all x1 -> x4, blocking collectives: 26.2 us -> 118 us  [exchange(): return lax.all_to_all(value, axes, split_axis=0, concat_axis=0, tiled=True)]
    unnamed x32 -> x19, local copies, waits for them, and re-layouts: 58.4 us -> 3.54 us
    all_to_all x2 -> x0, waiting for transfers between devices: 51 us -> none  [the longest x1 51 us: per_device(): lax.all_to_all(served.reshape(device_count, CAP, ROWS, half_width), 'dp',...]
    scatter x1 -> x0, local copies, waits for them, and re-layouts: 18.4 us -> none  [per_device(): jnp.zeros((slot_count, ROWS, half_width), jnp.float32).at[slot_index]]
    all_to_all x2 -> x0, starting transfers between devices: 18.3 us -> none  [the longest x1 10.3 us: per_device(): lax.all_to_all(outgoing.reshape(device_count, CAP, ROWS, half_width), 'dp...]
  transfers between devices with their start and end apart: 35 -> 3, of which waited for: 4 -> 3; matrix products, arithmetic and copies ran while one was open for 36% -> 0% of each run, Pallas kernels for 0% -> 1%
where the time goes in v1:
time: 141 us
  blocking collectives  118 us (84%)
  Pallas kernels  14.2 us (10%)
  waiting for transfers between devices  4.46 us (3%)
  local copies, waits for them, and re-layouts  3.54 us (3%)
    all_to_all x4, blocking collectives, exchange(): return lax.all_to_all(value, axes, split_axis=0, concat_axis=0, tiled=True)  118 us
    pallas_call x1, Pallas kernels, per_device(): call(weight_body, [((PLANE, Z_ROWS + PACK, HALF), BF16)], 'weight_gradien...  4.03 us
    unnamed x19, local copies, waits for them, and re-layouts  3.54 us
  transfers between devices with their start and end apart: 3, of which 3 were waited for; matrix products, arithmetic and copies ran while one was open for 0% of the time, Pallas kernels for 1%

profile of v1, /device:TPU:8, one launch (start us, length us, event | category | flops | bytes accessed | tf_op | source)
XLA Modules:
  0.0 140.8 jit_solution(4025433003976563592)
XLA Ops:
  0.7 0.1 pad_add_fusion.place
  0.7 1.7 %copy-done = bf16[1536,768]{1,0:T(8,128)(2,1)S(1)} copy-done((bf16[1536,768]{1,0:T(8,128)(2,1)S(1)}, bf16[1536,768]{1,0:T(8,128)(2,1)}, u32[]{:S(2)}) %copy-start) | copy-done | bytes 2359320
  2.4 1.0 copy-done.2
  3.4 0.7 copy-done.5
  4.1 2.8 %conv_and_other_half.1 = (bf16[256,768]{1,0:T(8,128)(2,1)S(1)}, f32[256,768]{1,0:T(8,128)}) custom-call(s32[2]{0:T(128)S(1)} %pad_add_fusion.place, bf16[256,768]{1,0:T(8,128)(2,1)S(1)} %bitcast.4, f32[7,768]{1,0:T(8,128)S(1)} %copy-done.5, bf16[1536,768]{1,0:T(8,128)(2,1)S(1)} %copy-done), custom_call_target="tpu_custom_call" | custom-call | flops 301989888 | bytes 1048576 | tf_op jit(solution)/shard_map/conv_and_other_half/pallas_call | solution.py:252
  6.9 0.1 copy.10.owner_ref
  7.1 0.0 copy-start.4
  7.1 1.1 own_half_and_requests.1
  8.2 1.4 collective-permute-done.other_ref
  9.6 1.8 %embedding.1 = (f32[256,768]{1,0:T(8,128)S(1)}, f32[8,768]{1,0:T(8,128)S(1)}, f32[128,1,896]{2,1,0:T(1,128)S(1)}) custom-call(f32[256,768]{1,0:T(8,128)S(1)} %get-tuple-element.17.own_ref, f32[256,768]{1,0:T(8,128)} %collective-permute-done.other_ref, bf16[256,768]{1,0:T(8,128)(2,1)S(1)} %bitcast.5, f32[128,128]{1,0:T(8,128)S(1)} %get-tuple-element.19.table_ref), custom_call_target="tpu_custom_call" | custom-call | bytes 1048576 | tf_op jit(solution)/shard_map/embedding/pallas_call | solution.py:270
  11.3 32.4 %all_to_all.20.recv_ref.first_ref = f32[128,1,896]{2,1,0:T(1,128)S(1)} all-to-all(f32[128,1,896]{2,1,0:T(1,128)S(1)} %get-tuple-element.20), channel_id=1, replica_groups=mesh['x'=4,'y'=4,'z'=8,'group'=2] {'x','y','z'}, dimensions={0} | all-to-all | bytes 917504 | tf_op jit(solution)/shard_map/all_to_all | solution.py:241
  43.8 0.9 inner_products.1.mine_ref
  44.7 0.1 collective-permute-start.1
  44.8 1.4 collective-permute-done.1.theirs_ref
  46.1 1.3 scores.1
  47.4 25.2 %all_to_all.21.recv_ref = f32[128,1,896]{2,1,0:T(1,128)S(1)} all-to-all(f32[128,1,896]{2,1,0:T(1,128)S(1)} %get-tuple-element.22), channel_id=1, replica_groups=mesh['x'=4,'y'=4,'z'=8,'group'=2] {'x','y','z'}, dimensions={0} | all-to-all | bytes 917504 | tf_op jit(solution)/shard_map/all_to_all | solution.py:241
  72.7 0.8 mixed_gradient.1
  73.4 0.1 collective-permute-start.2
  73.5 1.7 %collective-permute-done.2.theirs_ref = bf16[256,768]{1,0:T(8,128)(2,1)S(1)} collective-permute-done((bf16[256,768]{1,0:T(8,128)(2,1)S(1)}, bf16[256,768]{1,0:T(8,128)(2,1)S(1)}, u32[]{:S(2)}, u32[]{:S(2)}) %collective-permute-start.2) | collective-permute-done | bytes 393248 | tf_op jit(solution)/shard_map/ppermute | solution.py:301
  75.3 4.0 %weight_gradient.1 = bf16[16,112,768]{2,1,0:T(8,128)(2,1)} custom-call(s32[2]{0:T(128)S(1)} %pad_add_fusion.place, bf16[256,768]{1,0:T(8,128)(2,1)S(1)} %get-tuple-element.25.mine_ref, bf16[256,768]{1,0:T(8,128)(2,1)S(1)} %collective-permute-done.2.theirs_ref, bf16[256,768]{1,0:T(8,128)(2,1)S(1)} %get-tuple-element.16.hidden_ref, ...), custom_call_target="tpu_custom_call" | custom-call | bytes 1048576 | tf_op jit(solution)/shard_map/weight_gradient/pallas_call | solution.py:302
  79.3 41.3 %all_to_all.22.recv_ref = bf16[16,112,768]{2,1,0:T(8,128)(2,1)S(1)} all-to-all(bf16[16,112,768]{2,1,0:T(8,128)(2,1)} %weight_gradient.1), channel_id=1, replica_groups=mesh['x'=4,'y'=4,'z'=8,'group'=2] {'x','y'}, dimensions={0} | all-to-all | bytes 5505024 | tf_op jit(solution)/shard_map/all_to_all | solution.py:241
  120.5 0.4 sum_over_plane.1
  120.9 18.6 %all_to_all.23.recv_ref = f32[8,120,128]{2,1,0:T(8,128)S(1)} all-to-all(f32[8,120,128]{2,1,0:T(8,128)S(1)} %sum_over_plane.1), channel_id=1, replica_groups=mesh['x'=4,'y'=4,'z'=8,'group'=2] {'z'}, dimensions={0} | all-to-all | bytes 983040 | tf_op jit(solution)/shard_map/all_to_all | solution.py:241
  139.5 1.3 outputs.1
  (15 shorter events, 0.0 us)
Async XLA Ops:
  0.6 6.3 %copy-start.8 = (s32[128,1]{0,1:T(1,128)S(1)}, s32[128,1]{0,1:T(1,128)}, u32[]{:S(2)}) copy-start(s32[128,1]{0,1:T(1,128)} %param.12) | copy-start | bytes 1540
  0.6 6.4 %copy-start.7 = (s32[128]{0:T(128)S(1)}, s32[128]{0:T(128)}, u32[]{:S(2)}) copy-start(s32[128]{0:T(128)} %param.13) | copy-start | bytes 1540
  0.7 1.7 %copy-start = (bf16[1536,768]{1,0:T(8,128)(2,1)S(1)}, bf16[1536,768]{1,0:T(8,128)(2,1)}, u32[]{:S(2)}) copy-start(bf16[1536,768]{1,0:T(8,128)(2,1)} %w_ref.5) | copy-start | bytes 7077892
  2.4 1.0 copy-start.2
  3.4 0.7 copy-start.5
  4.1 2.9 %copy-start.1 = (bf16[1536,768]{1,0:T(8,128)(2,1)S(1)}, bf16[1536,768]{1,0:T(8,128)(2,1)}, u32[]{:S(2)}) copy-start(bf16[1536,768]{1,0:T(8,128)(2,1)} %w_ref.5) | copy-start | bytes 7077892
  4.1 5.4 %copy-start.3 = (bf16[1,256,768]{2,1,0:T(8,128)(2,1)S(1)}, bf16[1,256,768]{2,1,0:T(8,128)(2,1)}, u32[]{:S(2)}) copy-start(bf16[1,256,768]{2,1,0:T(8,128)(2,1)} %param.7) | copy-start | bytes 1179652
  6.9 2.6 %collective-permute-start = (f32[256,768]{1,0:T(8,128)}, f32[256,768]{1,0:T(8,128)}, u32[]{:S(2)}, u32[]{:S(2)}) collective-permute-start(f32[256,768]{1,0:T(8,128)} %get-tuple-element.18), channel_id=1, source_target_pairs={{0,1},{1,0},{2,3},{3,2},{4,5},{5,4},{6,7},{7,6},{8,9},{9,8},{10,11... | collective-permute-start | bytes 2359304 | tf_op jit(solution)/shard_map/ppermute | solution.py:261
  7.1 36.7 %copy-start.4 = (bf16[128,768]{1,0:T(8,128)(2,1)S(1)}, bf16[128,768]{1,0:T(8,128)(2,1)}, u32[]{:S(2)}) copy-start(bf16[128,768]{1,0:T(8,128)(2,1)} %bank_ref.5) | copy-start | bytes 589828
  7.1 36.7 %copy-start.6 = (bf16[1,768]{1,0:T(2,128)(2,1)S(1)}, bf16[1,768]{1,0:T(2,128)(2,1)}, u32[]{:S(2)}) copy-start(bf16[1,768]{1,0:T(2,128)(2,1)} %pos_ref.3) | copy-start | bytes 4612
  44.7 1.5 %collective-permute-start.1 = (f32[288,128]{1,0:T(8,128)S(1)}, f32[288,128]{1,0:T(8,128)S(1)}, u32[]{:S(2)}, u32[]{:S(2)}) collective-permute-start(f32[288,128]{1,0:T(8,128)S(1)} %inner_products.1.mine_ref), channel_id=1, source_target_pairs={{0,1},{1,0},{2,3},{3,2},{4,5},{5,4},{6,7},{7,6},{8,9},{9,8},{10,11... | collective-permute-start | bytes 442376 | tf_op jit(solution)/shard_map/ppermute | solution.py:280
  73.4 1.8 %collective-permute-start.2 = (bf16[256,768]{1,0:T(8,128)(2,1)S(1)}, bf16[256,768]{1,0:T(8,128)(2,1)S(1)}, u32[]{:S(2)}, u32[]{:S(2)}) collective-permute-start(bf16[256,768]{1,0:T(8,128)(2,1)S(1)} %get-tuple-element.25.mine_ref), channel_id=1, source_target_pairs={{0,1},{1,0},{2,3},{3,2},{4,5},{5,4},{6,7},{7,6},{8,9},{9,8},{10,11... | collective-permute-start | bytes 1179656 | tf_op jit(solution)/shard_map/ppermute | solution.py:301

commit v2 on v1

v2 whole, which is shorter than its diff:
```python
import jax
import jax.numpy as jnp
from jax import lax
from jax.experimental import pallas as pl
from jax.experimental.pallas import tpu as pltpu
from jax.sharding import PartitionSpec as P

KW = 7
LEN = 256
HALF = 768
N_DP = 128
NX, NY, NZ = 4, 4, 8
PLANE = NX * NY
ROWS = 8
OWN = 128
OUT_ROWS = 12
Z_ROWS = OUT_ROWS * NZ
PACK = 8
SLOT = 8
LANES = 128
COLS = HALF // LANES

TEMPER = 0.07
SCALE = 256.0
EPSILON = 1e-06
GELU_C = 0.7978845608028654
GELU_A = 0.044715
PRECISE = lax.Precision.HIGHEST
F32 = jnp.float32
BF16 = jnp.bfloat16

DP = "dp"
PLANES = [[(x * NY + y) * NZ + z for x in range(NX) for y in range(NY)] for z in range(NZ)]
LINES = [[p * NZ + z for z in range(NZ)] for p in range(PLANE)]
SWAP = [(0, 1), (1, 0)]
VMEM_BYTES = 20 * 2**20

NT = (((1,), (1,)), ((), ()))
NN = (((1,), (0,)), ((), ()))
TN = (((0,), (0,)), ((), ()))


def dot(a, b, dims, precision=None):
    return lax.dot_general(a, b, dims, precision=precision, preferred_element_type=F32)


def call(body, outs, name, scratch=(), scalars=0, n_in=0, flops=0, in_hbm=0):
    smem = [pl.BlockSpec(memory_space=pltpu.SMEM)] * scalars
    vmem = [pl.BlockSpec(memory_space=pltpu.VMEM)] * n_in
    return pl.pallas_call(
        body,
        out_shape=[jax.ShapeDtypeStruct(s, d) for s, d in outs],
        in_specs=smem + [pl.BlockSpec(memory_space=pltpu.HBM)] * in_hbm + vmem,
        out_specs=[pl.BlockSpec(memory_space=pltpu.VMEM)] * len(outs),
        scratch_shapes=list(scratch),
        compiler_params=pltpu.CompilerParams(vmem_limit_bytes=VMEM_BYTES),
        cost_estimate=pl.CostEstimate(flops=flops, bytes_accessed=1 << 20, transcendentals=0),
        name=name,
    )


def fill_padded(tokens_ref, pad):
    pad[0:8, :] = jnp.zeros((8, HALF), F32)
    pad[LEN + 8 : LEN + 16, :] = jnp.zeros((8, HALF), F32)
    for t in range(0, LEN, 32):
        pad[8 + t : 40 + t, :] = tokens_ref[t : t + 32, :].astype(F32)


def conv_body(
    place, tokens_hbm, dw_hbm, w_hbm, hidden_ref, other_ref, pad, tokens_ref, dw_ref, w_ref, sems
):
    start = pl.multiple_of((1 - place[0]) * HALF, HALF)
    copies = [
        pltpu.make_async_copy(tokens_hbm, tokens_ref, sems.at[0]),
        pltpu.make_async_copy(dw_hbm, dw_ref, sems.at[1]),
        pltpu.make_async_copy(w_hbm.at[pl.ds(start, HALF), :], w_ref, sems.at[2]),
    ]
    for copy in copies:
        copy.start()
    copies[0].wait()
    fill_padded(tokens_ref, pad)
    copies[1].wait()
    for t in range(0, LEN, 32):
        total = jnp.zeros((32, HALF), F32)
        for k in range(KW):
            total = total + dw_ref[k : k + 1, :] * pad[5 + k + t : 37 + k + t, :]
        hidden_ref[t : t + 32, :] = total.astype(BF16)
    copies[2].wait()
    other_ref[...] = dot(hidden_ref[...], w_ref[...], NT)


def own_body(place, hidden_ref, w_ref, owner_ref, block_ref, own_ref, table_ref):
    start = pl.multiple_of(place[0] * HALF, HALF)
    own_ref[...] = dot(hidden_ref[...], w_ref[pl.ds(start, HALF), :], NT)
    lane = lax.broadcasted_iota(jnp.int32, (OWN, LANES), 1)
    named = (owner_ref[...] == lane).astype(F32)
    blocks = jnp.broadcast_to(block_ref[...].astype(F32), (LANES, OWN)).T
    wanted = (blocks == lane.astype(F32)).astype(F32)
    table_ref[...] = dot(named.T.astype(BF16), wanted.astype(BF16), NN)


def embed_body(own_ref, other_ref, tokens_ref, table_ref, slope_ref, emb_ref, send_ref, stage):
    total = jnp.zeros((8, HALF), F32)
    for t in range(0, LEN, 32):
        x = own_ref[t : t + 32, :] + other_ref[t : t + 32, :]
        sq = x * x
        th = jnp.tanh(GELU_C * x * (1.0 + GELU_A * sq))
        half = 0.5 * (1.0 + th)
        slope_ref[t : t + 32, :] = half + (0.5 * GELU_C) * x * (1.0 - th * th) * (
            1.0 + (3.0 * GELU_A) * sq
        )
        y = tokens_ref[t : t + 32, :].astype(F32) + x * half
        total = total + (y[0:8] + y[8:16]) + (y[16:24] + y[24:32])
    emb = jnp.sum(total, axis=0, keepdims=True) * (1.0 / LEN)
    emb_ref[...] = jnp.broadcast_to(emb, (8, HALF))
    for c in range(COLS):
        block = jnp.broadcast_to(emb[:, c * LANES : (c + 1) * LANES], (N_DP, LANES))
        stage[pl.ds(c, N_DP, stride=SLOT), :] = block
    stage[pl.ds(COLS, N_DP, stride=SLOT), :] = table_ref[...]
    stage[pl.ds(COLS + 1, N_DP, stride=SLOT), :] = jnp.zeros((N_DP, LANES), F32)
    send_ref[...] = stage[...].astype(BF16)


def dots_body(recv_ref, bank_ref, emb_ref, pos_ref, packet_ref, first_ref, count_ref, stage):
    stage[...] = recv_ref[...].astype(F32)
    for c in range(COLS):
        first_ref[:, c * LANES : (c + 1) * LANES] = stage[pl.ds(c, N_DP, stride=SLOT), :]
    count_ref[...] = stage[pl.ds(COLS, N_DP, stride=SLOT), :]
    e = first_ref[...]
    key = bank_ref[...].astype(F32)
    packet_ref[0:OWN, :] = dot(bank_ref[...], e.astype(BF16), NT)
    ones = jnp.ones((8, HALF), F32)
    packet_ref[OWN : OWN + 8, :] = dot(ones, e * e, NT, PRECISE)
    ksq = jnp.sum(key * key, axis=1, keepdims=True)
    packet_ref[OWN + 8 : 2 * OWN + 8, :] = jnp.broadcast_to(ksq, (OWN, LANES))
    emb = emb_ref[0:1, :]
    pos = pos_ref[...].astype(F32)
    rows = (emb * emb, emb * pos, pos * pos)
    for i in range(3):
        value = jnp.sum(rows[i], axis=1, keepdims=True)
        packet_ref[2 * OWN + 8 + 8 * i : 2 * OWN + 16 + 8 * i, :] = jnp.broadcast_to(
            value, (8, LANES)
        )


PACKET = 2 * OWN + 32


def scores_body(
    place, mine_ref, theirs_ref, count_ref, bank_ref, send_ref, coef_ref, kcoef_ref, scal_ref, stage
):
    full = mine_ref[...] + theirs_ref[...]
    en = jnp.sqrt(full[OWN : OWN + 1] + EPSILON)
    kn = jnp.sqrt(full[OWN + 8 : 2 * OWN + 8] + EPSILON)
    scal_ref[...] = full[2 * OWN + 8 : PACKET]
    score = full[0:OWN] / (TEMPER * en * kn)
    count = count_ref[...].T
    row = lax.broadcasted_iota(jnp.int32, (OWN, LANES), 0)
    lane = lax.broadcasted_iota(jnp.int32, (OWN, LANES), 1)
    spread = (row // ROWS == lane).astype(F32)
    count = dot(spread.astype(BF16), count.astype(BF16), NN)
    count = count + (lane == place[1]).astype(F32)
    ec = count * jnp.exp(score)
    z = jnp.sum(ec, axis=0, keepdims=True)
    s = jnp.sum(ec * score, axis=0, keepdims=True)
    blend = ec / kn
    coef_ref[...] = (SCALE / TEMPER) * blend / en
    kcoef_ref[...] = SCALE * ec * score / (kn * kn)
    sums = dot(blend.T, bank_ref[...].astype(F32), NN, PRECISE)
    for c in range(COLS):
        stage[pl.ds(c, N_DP, stride=SLOT), :] = sums[:, c * LANES : (c + 1) * LANES]
    zs = jnp.zeros((OWN, LANES), F32)
    for i, value in enumerate((z, s)):
        upper = value.astype(BF16).astype(F32)
        zs = jnp.where(row == 2 * i, jnp.broadcast_to(upper, (OWN, LANES)), zs)
        zs = jnp.where(row == 2 * i + 1, jnp.broadcast_to(value - upper, (OWN, LANES)), zs)
    stage[pl.ds(COLS, N_DP, stride=SLOT), :] = zs.T
    stage[pl.ds(COLS + 1, N_DP, stride=SLOT), :] = jnp.zeros((N_DP, LANES), F32)
    send_ref[...] = stage[...].astype(BF16)


def grad_body(place, recv_ref, emb_ref, pos_ref, scal_ref, slope_ref, mixed_ref, z_ref):
    acc = jnp.zeros((2 * SLOT, LANES), F32)
    for i in range(0, N_DP * SLOT, 2 * SLOT):
        acc = acc + recv_ref[i : i + 2 * SLOT, :].astype(F32)
    acc = acc[0:SLOT] + acc[SLOT : 2 * SLOT]
    total = jnp.concatenate([acc[c : c + 1] for c in range(COLS)], axis=1)
    tail = acc[COLS : COLS + 1]
    esq = scal_ref[0:1, 0:1]
    inner = scal_ref[8:9, 0:1]
    psq = scal_ref[16:17, 0:1]
    en = jnp.sqrt(esq + EPSILON)
    pn = jnp.sqrt(psq + EPSILON)
    score = inner / (TEMPER * en * pn)
    hit = jnp.exp(score)
    z = tail[:, 0:1] + tail[:, 1:2] + hit
    s = tail[:, 2:3] + tail[:, 3:4] + hit * score
    row_weight = SCALE * (s / z - score)
    unit = emb_ref[0:1, :] / en
    pos = pos_ref[...].astype(F32)
    direction = (SCALE / TEMPER) * (total / z + ((hit / z - 1.0) / pn) * pos)
    grad = (direction - row_weight * unit) / en * (1.0 / LEN)
    for t in range(0, LEN, 32):
        mixed_ref[t : t + 32, :] = (slope_ref[t : t + 32, :] * grad).astype(BF16)
    upper = z.astype(BF16).astype(F32)
    lane = lax.broadcasted_iota(jnp.int32, (8, HALF), 1)
    line = jnp.where(lane == place[1], jnp.broadcast_to(upper, (8, HALF)), 0.0)
    z_ref[...] = jnp.where(lane == place[1] + LANES, jnp.broadcast_to(z - upper, (8, HALF)), line)


def weight_body(
    place, mine_ref, theirs_ref, hidden_ref, w_ref, tokens_ref, z_ref, send_ref, pad, small
):
    fill_padded(tokens_ref, pad)
    g = place[0]
    first = pl.multiple_of(g * HALF, HALF)
    second = pl.multiple_of((1 - g) * HALF, HALF)
    hidden_grad = dot(mine_ref[...], w_ref[pl.ds(first, HALF), :], NN)
    hidden_grad = hidden_grad + dot(theirs_ref[...], w_ref[pl.ds(second, HALF), :], NN)
    for k in range(KW):
        small[k : k + 1, :] = jnp.sum(
            hidden_grad * pad[5 + k : 5 + k + LEN, :], axis=0, keepdims=True
        )
    small[KW : KW + 1, :] = z_ref[0:1, :]
    extra = small[...]
    per = PLANE // 2
    for side, ref in ((g, mine_ref), (1 - g, theirs_ref)):
        product = dot(ref[...], hidden_ref[...], TN)
        for p in range(per):
            rows = product[p * Z_ROWS : (p + 1) * Z_ROWS, :]
            send_ref[side * per + p] = jnp.concatenate([rows, extra], axis=0).astype(BF16)


BLOCK = OUT_ROWS + 8


def plane_body(recv_ref, send_ref, total):
    for c in range(COLS):
        cols = slice(c * LANES, (c + 1) * LANES)
        acc = recv_ref[0, :, cols].astype(F32)
        for p in range(1, PLANE):
            acc = acc + recv_ref[p, :, cols].astype(F32)
        total[:, cols] = acc
    last = Z_ROWS + PACK - 1
    total[last : last + 1, 0:LANES] = (
        total[last : last + 1, 0:LANES] + total[last : last + 1, LANES : 2 * LANES]
    )
    for c in range(COLS):
        cols = slice(c * LANES, (c + 1) * LANES)
        for z in range(NZ):
            send_ref[z, c * BLOCK : c * BLOCK + OUT_ROWS, :] = total[
                z * OUT_ROWS : (z + 1) * OUT_ROWS, cols
            ]
            send_ref[z, c * BLOCK + OUT_ROWS : (c + 1) * BLOCK, :] = total[
                Z_ROWS : Z_ROWS + PACK, cols
            ]


def final_body(
    recv_ref, coef_ref, kcoef_ref, first_ref, bank_ref, bank_out, kernel_out, weight_out, total
):
    acc = recv_ref[0]
    for z in range(1, NZ):
        acc = acc + recv_ref[z]
    total[...] = acc
    for c in range(COLS):
        cols = slice(c * LANES, (c + 1) * LANES)
        base = c * BLOCK
        weight_out[:, cols] = total[base : base + OUT_ROWS, :] * (1.0 / N_DP)
        kernel_out[:, cols] = total[base + OUT_ROWS : base + OUT_ROWS + KW, :] * (1.0 / N_DP)
    inverse = 1.0 / total[BLOCK - 1 : BLOCK, :]
    coef = coef_ref[...] * inverse
    scale = jnp.sum(kcoef_ref[...] * inverse, axis=1, keepdims=True)
    product = dot(coef, first_ref[...], NN, PRECISE)
    bank_out[...] = product - scale * bank_ref[...].astype(F32)


def exchange(value, groups=None):
    return lax.all_to_all(
        value, DP, split_axis=0, concat_axis=0, tiled=True, axis_index_groups=groups
    )


def exchange_slots(value):
    return exchange(value.reshape(N_DP, SLOT, LANES)).reshape(N_DP * SLOT, LANES)


def per_device(tokens_in, dw_kernel, point_weight, positive_emb, bank, neg_owner, neg_block):
    tokens = tokens_in.reshape(LEN, HALF)
    g = lax.axis_index("group")
    d = lax.axis_index(DP)
    place = jnp.stack([g, d]).astype(jnp.int32)
    pad = pltpu.VMEM((LEN + 16, HALF), F32)
    stage = pltpu.VMEM((N_DP * SLOT, LANES), F32)
    flops = 2 * LEN * HALF * HALF

    hidden, other = call(
        conv_body,
        [((LEN, HALF), BF16), ((LEN, HALF), F32)],
        "conv_and_other_half",
        [
            pad,
            pltpu.VMEM((LEN, HALF), BF16),
            pltpu.VMEM((KW, HALF), F32),
            pltpu.VMEM((HALF, HALF), BF16),
            pltpu.SemaphoreType.DMA((3,)),
        ],
        scalars=1,
        in_hbm=3,
        flops=flops,
    )(place, tokens, dw_kernel, point_weight)
    theirs = lax.ppermute(other, "group", SWAP)
    own, table = call(
        own_body,
        [((LEN, HALF), F32), ((N_DP, LANES), F32)],
        "own_half_and_requests",
        scalars=1,
        n_in=4,
        flops=flops,
    )(place, hidden, point_weight, neg_owner, neg_block.reshape(1, OWN))
    slope, emb, send = call(
        embed_body,
        [((LEN, HALF), F32), ((8, HALF), F32), ((N_DP * SLOT, LANES), BF16)],
        "embedding",
        [stage],
        n_in=4,
    )(own, theirs, tokens, table)
    gathered = exchange_slots(send)
    packet, first, count = call(
        dots_body,
        [((PACKET, LANES), F32), ((N_DP, HALF), F32), ((N_DP, LANES), F32)],
        "inner_products",
        [stage],
        n_in=4,
    )(gathered, bank, emb, positive_emb)
    packet_theirs = lax.ppermute(packet, "group", SWAP)
    send, coef, kcoef, scal = call(
        scores_body,
        [
            ((N_DP * SLOT, LANES), BF16),
            ((OWN, LANES), F32),
            ((OWN, LANES), F32),
            ((24, LANES), F32),
        ],
        "scores",
        [stage],
        scalars=1,
        n_in=4,
    )(place, packet, packet_theirs, count, bank)
    sums = exchange_slots(send)
    mixed, z = call(
        grad_body,
        [((LEN, HALF), BF16), ((8, HALF), F32)],
        "mixed_gradient",
        scalars=1,
        n_in=5,
    )(place, sums, emb, positive_emb, scal, slope)
    mixed_theirs = lax.ppermute(mixed, "group", SWAP)
    (send,) = call(
        weight_body,
        [((PLANE, Z_ROWS + PACK, HALF), BF16)],
        "weight_gradient",
        [pad, pltpu.VMEM((8, HALF), F32)],
        scalars=1,
        n_in=6,
    )(place, mixed, mixed_theirs, hidden, point_weight, tokens, z)
    planes = exchange(send, PLANES)
    (send,) = call(
        plane_body,
        [((NZ, COLS * BLOCK, LANES), F32)],
        "sum_over_plane",
        [pltpu.VMEM((Z_ROWS + PACK, HALF), F32)],
        n_in=1,
    )(planes)
    lines = exchange(send, LINES)
    return tuple(
        call(
            final_body,
            [((OWN, HALF), F32), ((KW, HALF), F32), ((OUT_ROWS, HALF), F32)],
            "outputs",
            [pltpu.VMEM((COLS * BLOCK, LANES), F32)],
            n_in=5,
        )(lines, coef, kcoef, first, bank)
    )


def solution(mesh):
    in_specs = (
        P(DP, None, "group"),
        P(None, "group"),
        P(None, "group"),
        P(DP, "group"),
        P(DP, "group"),
        P(DP, None),
        P(DP),
    )
    out_specs = (P(DP, "group"), P(None, "group"), P(DP, "group"))
    return jax.shard_map(
        per_device, mesh=mesh, in_specs=in_specs, out_specs=out_specs, check_vma=False
    )
```

time: 141 us -> 129 us (0.915)
  blocking collectives: 118 us -> 106 us
    all_to_all x4, blocking collectives: 118 us -> 106 us  [exchange(): lax.all_to_all(value, DP, split_axis=0, concat_axis=0, tiled=True, axis_i...]
    pallas_call x1, Pallas kernels: 4.03 us -> 2.43 us  [per_device(): call(weight_body, [((PLANE, Z_ROWS + PACK, HALF), BF16)], 'weight_gradien...]
where the time goes in v2:
time: 129 us; the launch traced here: 128 us
  blocking collectives  106 us (82%)
  Pallas kernels  13.3 us (10%)
  waiting for transfers between devices  4.45 us (3%)
  local copies, waits for them, and re-layouts  3.54 us (3%)
    all_to_all x4, blocking collectives, exchange(): lax.all_to_all(value, DP, split_axis=0, concat_axis=0, tiled=True, axis_i...  106 us
    pallas_call x1, Pallas kernels, per_device(): call(conv_body, [((LEN, HALF), BF16), ((LEN, HALF), F32)], 'conv_and_othe...  3.56 us
    unnamed x19, local copies, waits for them, and re-layouts  3.54 us
  transfers between devices with their start and end apart: 3, of which 3 were waited for; matrix products, arithmetic and copies ran while one was open for 0% of the time, Pallas kernels for 1%

profile of v2, /device:TPU:8, one launch (start us, length us, event | category | flops | bytes accessed | tf_op | source)
XLA Modules:
  0.0 128.2 jit_solution(15548513484544407696)
XLA Ops:
  0.7 0.1 pad_add_fusion.place
  0.7 1.7 %copy-done = bf16[1536,768]{1,0:T(8,128)(2,1)S(1)} copy-done((bf16[1536,768]{1,0:T(8,128)(2,1)S(1)}, bf16[1536,768]{1,0:T(8,128)(2,1)}, u32[]{:S(2)}) %copy-start) | copy-done | bytes 2359320
  2.4 1.0 copy-done.2
  3.4 0.7 copy-done.5
  4.1 3.6 %conv_and_other_half.1 = (bf16[256,768]{1,0:T(8,128)(2,1)S(1)}, f32[256,768]{1,0:T(8,128)}) custom-call(s32[2]{0:T(128)S(1)} %pad_add_fusion.place, bf16[256,768]{1,0:T(8,128)(2,1)S(1)} %bitcast.8, f32[7,768]{1,0:T(8,128)S(1)} %copy-done.5, bf16[1536,768]{1,0:T(8,128)(2,1)S(1)} %copy-done), custom_call_target="tpu_custom_call" | custom-call | flops 301989888 | bytes 1048576 | tf_op jit(solution)/shard_map/conv_and_other_half/pallas_call | solution.py:297
  7.7 0.1 collective-permute-start
  7.8 0.1 copy.10.owner_ref
  8.0 1.1 own_half_and_requests.1
  9.0 1.4 %collective-permute-done.other_ref = f32[256,768]{1,0:T(8,128)} collective-permute-done((f32[256,768]{1,0:T(8,128)}, f32[256,768]{1,0:T(8,128)}, u32[]{:S(2)}, u32[]{:S(2)}) %collective-permute-start) | collective-permute-done | bytes 786464 | tf_op jit(solution)/shard_map/ppermute | solution.py:312
  10.4 1.9 %embedding.1 = (f32[256,768]{1,0:T(8,128)S(1)}, f32[8,768]{1,0:T(8,128)S(1)}, bf16[1024,128]{1,0:T(8,128)(2,1)S(1)}) custom-call(f32[256,768]{1,0:T(8,128)S(1)} %get-tuple-element.20.own_ref, f32[256,768]{1,0:T(8,128)} %collective-permute-done.other_ref, bf16[256,768]{1,0:T(8,128)(2,1)S(1)} %bitcast.9, f32[128,128]{1,0:T(8,128)S(1)} %get-tuple-element.22.table_ref), custom_call_target="tpu_custom_call" | custom-call | bytes 1048576 | tf_op jit(solution)/shard_map/embedding/pallas_call | solution.py:321
  12.4 28.9 %all_to_all.20 = bf16[128,8,128]{2,1,0:T(8,128)(2,1)S(1)} all-to-all(bf16[128,8,128]{2,1,0:T(8,128)(2,1)S(1)} %bitcast.14), channel_id=1, replica_groups=mesh['dp'=128,'group'=2] {'dp'}, dimensions={0} | all-to-all | bytes 524288 | tf_op jit(solution)/shard_map/all_to_all | solution.py:279
  41.3 0.6 inner_products.1
  41.9 0.1 collective-permute-start.1
  41.9 1.4 %collective-permute-done.1.theirs_ref = f32[288,128]{1,0:T(8,128)S(1)} collective-permute-done((f32[288,128]{1,0:T(8,128)S(1)}, f32[288,128]{1,0:T(8,128)S(1)}, u32[]{:S(2)}, u32[]{:S(2)}) %collective-permute-start.1) | collective-permute-done | bytes 147488 | tf_op jit(solution)/shard_map/ppermute | solution.py:336
  43.3 1.3 %scores.1 = (bf16[1024,128]{1,0:T(8,128)(2,1)S(1)}, f32[128,128]{1,0:T(8,128)S(1)}, f32[128,128]{1,0:T(8,128)S(1)}, f32[24,128]{1,0:T(8,128)S(1)}) custom-call(s32[2]{0:T(128)S(1)} %pad_add_fusion.place, f32[288,128]{1,0:T(8,128)S(1)} %get-tuple-element.25.mine_ref, f32[288,128]{1,0:T(8,128)S(1)} %collective-permute-done.1.theirs_ref, ...), custom_call_target="tpu_custom_call" | custom-call | bytes 1048576 | tf_op jit(solution)/shard_map/scores/pallas_call | solution.py:337
  44.6 21.1 %all_to_all.21 = bf16[128,8,128]{2,1,0:T(8,128)(2,1)S(1)} all-to-all(bf16[128,8,128]{2,1,0:T(8,128)(2,1)S(1)} %bitcast.13), channel_id=1, replica_groups=mesh['dp'=128,'group'=2] {'dp'}, dimensions={0} | all-to-all | bytes 524288 | tf_op jit(solution)/shard_map/all_to_all | solution.py:279
  65.7 0.9 mixed_gradient.1
  66.5 0.1 collective-permute-start.2
  66.6 1.7 %collective-permute-done.2.theirs_ref = bf16[256,768]{1,0:T(8,128)(2,1)S(1)} collective-permute-done((bf16[256,768]{1,0:T(8,128)(2,1)S(1)}, bf16[256,768]{1,0:T(8,128)(2,1)S(1)}, u32[]{:S(2)}, u32[]{:S(2)}) %collective-permute-start.2) | collective-permute-done | bytes 393248 | tf_op jit(solution)/shard_map/ppermute | solution.py:358
  68.3 2.4 %weight_gradient.1 = bf16[16,104,768]{2,1,0:T(8,128)(2,1)S(1)} custom-call(s32[2]{0:T(128)S(1)} %pad_add_fusion.place, bf16[256,768]{1,0:T(8,128)(2,1)S(1)} %get-tuple-element.30.mine_ref, bf16[256,768]{1,0:T(8,128)(2,1)S(1)} %collective-permute-done.2.theirs_ref, bf16[256,768]{1,0:T(8,128)(2,1)S(1)} %get-tuple-element.19.hidden_ref, ...), custom_call_target="tpu_custom_call" | custom-call | bytes 1048576 | tf_op jit(solution)/shard_map/weight_gradient/pallas_call | solution.py:359
  70.8 37.6 %all_to_all.22.recv_ref = bf16[16,104,768]{2,1,0:T(8,128)(2,1)S(1)} all-to-all(bf16[16,104,768]{2,1,0:T(8,128)(2,1)S(1)} %weight_gradient.1), channel_id=1, replica_groups={{0,16,32,48,64,80,96,112,128,144,160,176,192,208,224,240},{2,18,34,50,6..., dimensions={0} | all-to-all | bytes 5111808 | tf_op jit(solution)/shard_map/all_to_all | solution.py:279
  108.4 0.3 sum_over_plane.1
  108.7 18.2 %all_to_all.23.recv_ref = f32[8,120,128]{2,1,0:T(8,128)S(1)} all-to-all(f32[8,120,128]{2,1,0:T(8,128)S(1)} %sum_over_plane.1), channel_id=1, replica_groups={{0,2,4,6,8,10,12,14},{16,18,20,22,24,26,28,30},{32,34,36,38,40,42,44,46..., dimensions={0} | all-to-all | bytes 983040 | tf_op jit(solution)/shard_map/all_to_all | solution.py:279
  126.9 1.2 outputs.1
  (15 shorter events, 0.0 us)
Async XLA Ops:
  0.6 7.2 %copy-start.8 = (s32[128,1]{0,1:T(1,128)S(1)}, s32[128,1]{0,1:T(1,128)}, u32[]{:S(2)}) copy-start(s32[128,1]{0,1:T(1,128)} %param.12) | copy-start | bytes 1540
  0.6 7.3 %copy-start.7 = (s32[128]{0:T(128)S(1)}, s32[128]{0:T(128)}, u32[]{:S(2)}) copy-start(s32[128]{0:T(128)} %param.13) | copy-start | bytes 1540
  0.7 1.7 %copy-start = (bf16[1536,768]{1,0:T(8,128)(2,1)S(1)}, bf16[1536,768]{1,0:T(8,128)(2,1)}, u32[]{:S(2)}) copy-start(bf16[1536,768]{1,0:T(8,128)(2,1)} %w_ref.3) | copy-start | bytes 7077892
  2.4 1.0 copy-start.2
  3.4 0.7 copy-start.5
  4.1 3.8 %copy-start.1 = (bf16[1536,768]{1,0:T(8,128)(2,1)S(1)}, bf16[1536,768]{1,0:T(8,128)(2,1)}, u32[]{:S(2)}) copy-start(bf16[1536,768]{1,0:T(8,128)(2,1)} %w_ref.3) | copy-start | bytes 7077892
  4.1 6.3 %copy-start.3 = (bf16[1,256,768]{2,1,0:T(8,128)(2,1)S(1)}, bf16[1,256,768]{2,1,0:T(8,128)(2,1)}, u32[]{:S(2)}) copy-start(bf16[1,256,768]{2,1,0:T(8,128)(2,1)} %param.7) | copy-start | bytes 1179652
  7.7 2.7 %collective-permute-start = (f32[256,768]{1,0:T(8,128)}, f32[256,768]{1,0:T(8,128)}, u32[]{:S(2)}, u32[]{:S(2)}) collective-permute-start(f32[256,768]{1,0:T(8,128)} %get-tuple-element.21), channel_id=1, source_target_pairs={{0,1},{1,0},{2,3},{3,2},{4,5},{5,4},{6,7},{7,6},{8,9},{9,8},{10,11... | collective-permute-start | bytes 2359304 | tf_op jit(solution)/shard_map/ppermute | solution.py:312
  7.9 33.4 %copy-start.4 = (bf16[128,768]{1,0:T(8,128)(2,1)S(1)}, bf16[128,768]{1,0:T(8,128)(2,1)}, u32[]{:S(2)}) copy-start(bf16[128,768]{1,0:T(8,128)(2,1)} %bank_ref.5) | copy-start | bytes 589828
  8.0 33.4 %copy-start.6 = (bf16[1,768]{1,0:T(2,128)(2,1)S(1)}, bf16[1,768]{1,0:T(2,128)(2,1)}, u32[]{:S(2)}) copy-start(bf16[1,768]{1,0:T(2,128)(2,1)} %pos_ref.3) | copy-start | bytes 4612
  41.9 1.4 %collective-permute-start.1 = (f32[288,128]{1,0:T(8,128)S(1)}, f32[288,128]{1,0:T(8,128)S(1)}, u32[]{:S(2)}, u32[]{:S(2)}) collective-permute-start(f32[288,128]{1,0:T(8,128)S(1)} %get-tuple-element.25.mine_ref), channel_id=1, source_target_pairs={{0,1},{1,0},{2,3},{3,2},{4,5},{5,4},{6,7},{7,6},{8,9},{9,8},{10,11... | collective-permute-start | bytes 442376 | tf_op jit(solution)/shard_map/ppermute | solution.py:336
  66.5 1.8 %collective-permute-start.2 = (bf16[256,768]{1,0:T(8,128)(2,1)S(1)}, bf16[256,768]{1,0:T(8,128)(2,1)S(1)}, u32[]{:S(2)}, u32[]{:S(2)}) collective-permute-start(bf16[256,768]{1,0:T(8,128)(2,1)S(1)} %get-tuple-element.30.mine_ref), channel_id=1, source_target_pairs={{0,1},{1,0},{2,3},{3,2},{4,5},{5,4},{6,7},{7,6},{8,9},{9,8},{10,11... | collective-permute-start | bytes 1179656 | tf_op jit(solution)/shard_map/ppermute | solution.py:358

commit v3 on v2

--- a/solution.py
+++ b/solution.py
@@ -44,17 +44,17 @@
     return lax.dot_general(a, b, dims, precision=precision, preferred_element_type=F32)
 
 
-def call(body, outs, name, scratch=(), scalars=0, n_in=0, flops=0, in_hbm=0):
+def call(body, outs, name, scratch=(), scalars=0, n_in=0, flops=0, moved=1 << 20):
     smem = [pl.BlockSpec(memory_space=pltpu.SMEM)] * scalars
     vmem = [pl.BlockSpec(memory_space=pltpu.VMEM)] * n_in
     return pl.pallas_call(
         body,
         out_shape=[jax.ShapeDtypeStruct(s, d) for s, d in outs],
-        in_specs=smem + [pl.BlockSpec(memory_space=pltpu.HBM)] * in_hbm + vmem,
+        in_specs=smem + vmem,
         out_specs=[pl.BlockSpec(memory_space=pltpu.VMEM)] * len(outs),
         scratch_shapes=list(scratch),
         compiler_params=pltpu.CompilerParams(vmem_limit_bytes=VMEM_BYTES),
-        cost_estimate=pl.CostEstimate(flops=flops, bytes_accessed=1 << 20, transcendentals=0),
+        cost_estimate=pl.CostEstimate(flops=flops, bytes_accessed=moved, transcendentals=0),
         name=name,
     )
 
@@ -66,27 +66,18 @@
         pad[8 + t : 40 + t, :] = tokens_ref[t : t + 32, :].astype(F32)
 
 
-def conv_body(
-    place, tokens_hbm, dw_hbm, w_hbm, hidden_ref, other_ref, pad, tokens_ref, dw_ref, w_ref, sems
-):
-    start = pl.multiple_of((1 - place[0]) * HALF, HALF)
-    copies = [
-        pltpu.make_async_copy(tokens_hbm, tokens_ref, sems.at[0]),
-        pltpu.make_async_copy(dw_hbm, dw_ref, sems.at[1]),
-        pltpu.make_async_copy(w_hbm.at[pl.ds(start, HALF), :], w_ref, sems.at[2]),
-    ]
-    for copy in copies:
-        copy.start()
-    copies[0].wait()
+def conv_body(tokens_ref, dw_ref, hidden_ref, pad):
     fill_padded(tokens_ref, pad)
-    copies[1].wait()
     for t in range(0, LEN, 32):
         total = jnp.zeros((32, HALF), F32)
         for k in range(KW):
             total = total + dw_ref[k : k + 1, :] * pad[5 + k + t : 37 + k + t, :]
         hidden_ref[t : t + 32, :] = total.astype(BF16)
-    copies[2].wait()
-    other_ref[...] = dot(hidden_ref[...], w_ref[...], NT)
+
+
+def other_body(place, hidden_ref, w_ref, other_ref):
+    start = pl.multiple_of((1 - place[0]) * HALF, HALF)
+    other_ref[...] = dot(hidden_ref[...], w_ref[pl.ds(start, HALF), :], NT)
 
 
 def own_body(place, hidden_ref, w_ref, owner_ref, block_ref, own_ref, table_ref):
@@ -208,67 +199,69 @@
     z_ref[...] = jnp.where(lane == place[1] + LANES, jnp.broadcast_to(z - upper, (8, HALF)), line)
 
 
+def mine_body(place, mine_ref, hidden_ref, w_ref, product_ref, part_ref):
+    g = place[0]
+    first = pl.multiple_of(g * HALF, HALF)
+    part_ref[...] = dot(mine_ref[...], w_ref[pl.ds(first, HALF), :], NN)
+    product_ref[...] = dot(mine_ref[...], hidden_ref[...], TN)
+
+
 def weight_body(
-    place, mine_ref, theirs_ref, hidden_ref, w_ref, tokens_ref, z_ref, send_ref, pad, small
+    place, theirs_ref, hidden_ref, w_ref, tokens_ref, z_ref, part_ref, mine_ref, send_ref, pad, small
 ):
     fill_padded(tokens_ref, pad)
     g = place[0]
-    first = pl.multiple_of(g * HALF, HALF)
     second = pl.multiple_of((1 - g) * HALF, HALF)
-    hidden_grad = dot(mine_ref[...], w_ref[pl.ds(first, HALF), :], NN)
-    hidden_grad = hidden_grad + dot(theirs_ref[...], w_ref[pl.ds(second, HALF), :], NN)
+    hidden_grad = part_ref[...] + dot(theirs_ref[...], w_ref[pl.ds(second, HALF), :], NN)
     for k in range(KW):
         small[k : k + 1, :] = jnp.sum(
             hidden_grad * pad[5 + k : 5 + k + LEN, :], axis=0, keepdims=True
         )
     small[KW : KW + 1, :] = z_ref[0:1, :]
     extra = small[...]
+    product = dot(theirs_ref[...], hidden_ref[...], TN)
     per = PLANE // 2
-    for side, ref in ((g, mine_ref), (1 - g, theirs_ref)):
-        product = dot(ref[...], hidden_ref[...], TN)
-        for p in range(per):
-            rows = product[p * Z_ROWS : (p + 1) * Z_ROWS, :]
+    for p in range(per):
+        span = slice(p * Z_ROWS, (p + 1) * Z_ROWS)
+        for side, rows in ((g, mine_ref[span, :]), (1 - g, product[span, :])):
             send_ref[side * per + p] = jnp.concatenate([rows, extra], axis=0).astype(BF16)
 
 
 BLOCK = OUT_ROWS + 8
 
 
-def plane_body(recv_ref, send_ref, total):
+def plane_body(recv_ref, send_ref, total, stage):
     for c in range(COLS):
         cols = slice(c * LANES, (c + 1) * LANES)
         acc = recv_ref[0, :, cols].astype(F32)
         for p in range(1, PLANE):
             acc = acc + recv_ref[p, :, cols].astype(F32)
         total[:, cols] = acc
-    last = Z_ROWS + PACK - 1
-    total[last : last + 1, 0:LANES] = (
-        total[last : last + 1, 0:LANES] + total[last : last + 1, LANES : 2 * LANES]
-    )
     for c in range(COLS):
         cols = slice(c * LANES, (c + 1) * LANES)
         for z in range(NZ):
-            send_ref[z, c * BLOCK : c * BLOCK + OUT_ROWS, :] = total[
+            stage[z, c * BLOCK : c * BLOCK + OUT_ROWS, :] = total[
                 z * OUT_ROWS : (z + 1) * OUT_ROWS, cols
             ]
-            send_ref[z, c * BLOCK + OUT_ROWS : (c + 1) * BLOCK, :] = total[
+            stage[z, c * BLOCK + OUT_ROWS : (c + 1) * BLOCK, :] = total[
                 Z_ROWS : Z_ROWS + PACK, cols
             ]
+    send_ref[...] = stage[...].astype(BF16)
 
 
 def final_body(
     recv_ref, coef_ref, kcoef_ref, first_ref, bank_ref, bank_out, kernel_out, weight_out, total
 ):
-    acc = recv_ref[0]
+    acc = recv_ref[0].astype(F32)
     for z in range(1, NZ):
-        acc = acc + recv_ref[z]
+        acc = acc + recv_ref[z].astype(F32)
     total[...] = acc
     for c in range(COLS):
         cols = slice(c * LANES, (c + 1) * LANES)
         base = c * BLOCK
         weight_out[:, cols] = total[base : base + OUT_ROWS, :] * (1.0 / N_DP)
         kernel_out[:, cols] = total[base + OUT_ROWS : base + OUT_ROWS + KW, :] * (1.0 / N_DP)
-    inverse = 1.0 / total[BLOCK - 1 : BLOCK, :]
+    inverse = 1.0 / (total[BLOCK - 1 : BLOCK, :] + total[2 * BLOCK - 1 : 2 * BLOCK, :])
     coef = coef_ref[...] * inverse
     scale = jnp.sum(kcoef_ref[...] * inverse, axis=1, keepdims=True)
     product = dot(coef, first_ref[...], NN, PRECISE)
@@ -294,21 +287,12 @@
     stage = pltpu.VMEM((N_DP * SLOT, LANES), F32)
     flops = 2 * LEN * HALF * HALF
 
-    hidden, other = call(
-        conv_body,
-        [((LEN, HALF), BF16), ((LEN, HALF), F32)],
-        "conv_and_other_half",
-        [
-            pad,
-            pltpu.VMEM((LEN, HALF), BF16),
-            pltpu.VMEM((KW, HALF), F32),
-            pltpu.VMEM((HALF, HALF), BF16),
-            pltpu.SemaphoreType.DMA((3,)),
-        ],
-        scalars=1,
-        in_hbm=3,
-        flops=flops,
-    )(place, tokens, dw_kernel, point_weight)
+    (hidden,) = call(conv_body, [((LEN, HALF), BF16)], "convolution", [pad], n_in=2, moved=16 << 20)(
+        tokens, dw_kernel
+    )
+    (other,) = call(
+        other_body, [((LEN, HALF), F32)], "other_half", scalars=1, n_in=2, flops=flops
+    )(place, hidden, point_weight)
     theirs = lax.ppermute(other, "group", SWAP)
     own, table = call(
         own_body,
@@ -356,20 +340,29 @@
         n_in=5,
     )(place, sums, emb, positive_emb, scal, slope)
     mixed_theirs = lax.ppermute(mixed, "group", SWAP)
+    product, part = call(
+        mine_body,
+        [((HALF, HALF), F32), ((LEN, HALF), F32)],
+        "weight_gradient_own_half",
+        scalars=1,
+        n_in=3,
+        flops=2 * flops,
+    )(place, mixed, hidden, point_weight)
     (send,) = call(
         weight_body,
         [((PLANE, Z_ROWS + PACK, HALF), BF16)],
         "weight_gradient",
         [pad, pltpu.VMEM((8, HALF), F32)],
         scalars=1,
-        n_in=6,
-    )(place, mixed, mixed_theirs, hidden, point_weight, tokens, z)
+        n_in=7,
+        flops=2 * flops,
+    )(place, mixed_theirs, hidden, point_weight, tokens, z, part, product)
     planes = exchange(send, PLANES)
     (send,) = call(
         plane_body,
-        [((NZ, COLS * BLOCK, LANES), F32)],
+        [((NZ, COLS * BLOCK, LANES), BF16)],
         "sum_over_plane",
-        [pltpu.VMEM((Z_ROWS + PACK, HALF), F32)],
+        [pltpu.VMEM((Z_ROWS + PACK, HALF), F32), pltpu.VMEM((NZ, COLS * BLOCK, LANES), F32)],
         n_in=1,
     )(planes)
     lines = exchange(send, LINES)

time: 129 us -> 122 us (0.946)
  blocking collectives: 106 us -> 101 us
  waiting for transfers between devices: 4.45 us -> 3.14 us
    all_to_all x4, blocking collectives: 106 us -> 101 us  [exchange(): lax.all_to_all(value, DP, split_axis=0, concat_axis=0, tiled=True, axis_i...]
    ppermute x1, waiting for transfers between devices: 1.71 us -> 0.38 us  [per_device(): mixed_theirs = lax.ppermute(mixed, 'group', SWAP)]
    pallas_call x2 -> x4, Pallas kernels: 3.9 us -> 4.65 us  [the longest x1 1.95 us: per_device(): call(other_body, [((LEN, HALF), F32)], 'other_half', scalars=1, n_in=2, f...]
  transfers between devices with their start and end apart: 3 -> 3, of which waited for: 3 -> 3; matrix products, arithmetic and copies ran while one was open for 0% -> 0% of each run, Pallas kernels for 1% -> 2%
where the time goes in v3:
time: 122 us
  blocking collectives  101 us (83%)
  Pallas kernels  13.7 us (11%)
  local copies, waits for them, and re-layouts  3.53 us (3%)
  waiting for transfers between devices  3.14 us (3%)
    all_to_all x4, blocking collectives, exchange(): lax.all_to_all(value, DP, split_axis=0, concat_axis=0, tiled=True, axis_i...  101 us
    unnamed x19, local copies, waits for them, and re-layouts  3.53 us
  transfers between devices with their start and end apart: 3, of which 3 were waited for; matrix products, arithmetic and copies ran while one was open for 0% of the time, Pallas kernels for 2%

profile of v3, /device:TPU:8, one launch (start us, length us, event | category | flops | bytes accessed | tf_op | source)
XLA Modules:
  0.0 121.9 jit_solution(11312274305407631983)
XLA Ops:
  0.7 0.1 pad_add_fusion.place
  0.7 1.0 copy-done.2
  1.7 0.7 copy-done.5
  2.5 1.0 convolution.1.hidden_ref
  3.5 1.7 %copy-done = bf16[1536,768]{1,0:T(8,128)(2,1)S(1)} copy-done((bf16[1536,768]{1,0:T(8,128)(2,1)S(1)}, bf16[1536,768]{1,0:T(8,128)(2,1)}, u32[]{:S(2)}) %copy-start) | copy-done | bytes 2359320
  5.2 2.0 %other_half.1 = f32[256,768]{1,0:T(8,128)} custom-call(s32[2]{0:T(128)S(1)} %pad_add_fusion.place, bf16[256,768]{1,0:T(8,128)(2,1)S(1)} %convolution.1.hidden_ref, bf16[1536,768]{1,0:T(8,128)(2,1)S(1)} %copy-done), custom_call_target="tpu_custom_call" | custom-call | flops 301989888 | bytes 1048576 | tf_op jit(solution)/shard_map/other_half/pallas_call | solution.py:293
  7.1 0.1 copy.10.owner_ref
  7.3 1.1 own_half_and_requests.1
  8.3 1.4 %collective-permute-done.other_ref = f32[256,768]{1,0:T(8,128)} collective-permute-done((f32[256,768]{1,0:T(8,128)}, f32[256,768]{1,0:T(8,128)}, u32[]{:S(2)}, u32[]{:S(2)}) %collective-permute-start) | collective-permute-done | bytes 786464 | tf_op jit(solution)/shard_map/ppermute | solution.py:296
  9.8 1.9 %embedding.1 = (f32[256,768]{1,0:T(8,128)S(1)}, f32[8,768]{1,0:T(8,128)S(1)}, bf16[1024,128]{1,0:T(8,128)(2,1)S(1)}) custom-call(f32[256,768]{1,0:T(8,128)S(1)} %get-tuple-element.19.own_ref, f32[256,768]{1,0:T(8,128)} %collective-permute-done.other_ref, bf16[256,768]{1,0:T(8,128)(2,1)S(1)} %bitcast.9, f32[128,128]{1,0:T(8,128)S(1)} %get-tuple-element.20.table_ref), custom_call_target="tpu_custom_call" | custom-call | bytes 1048576 | tf_op jit(solution)/shard_map/embedding/pallas_call | solution.py:305
  11.7 28.9 %all_to_all.20 = bf16[128,8,128]{2,1,0:T(8,128)(2,1)S(1)} all-to-all(bf16[128,8,128]{2,1,0:T(8,128)(2,1)S(1)} %bitcast.14), channel_id=1, replica_groups=mesh['dp'=128,'group'=2] {'dp'}, dimensions={0} | all-to-all | bytes 524288 | tf_op jit(solution)/shard_map/all_to_all | solution.py:272
  40.6 0.6 inner_products.1
  41.3 1.4 %collective-permute-done.1.theirs_ref = f32[288,128]{1,0:T(8,128)S(1)} collective-permute-done((f32[288,128]{1,0:T(8,128)S(1)}, f32[288,128]{1,0:T(8,128)S(1)}, u32[]{:S(2)}, u32[]{:S(2)}) %collective-permute-start.1) | collective-permute-done | bytes 147488 | tf_op jit(solution)/shard_map/ppermute | solution.py:320
  42.6 1.3 %scores.1 = (bf16[1024,128]{1,0:T(8,128)(2,1)S(1)}, f32[128,128]{1,0:T(8,128)S(1)}, f32[128,128]{1,0:T(8,128)S(1)}, f32[24,128]{1,0:T(8,128)S(1)}) custom-call(s32[2]{0:T(128)S(1)} %pad_add_fusion.place, f32[288,128]{1,0:T(8,128)S(1)} %get-tuple-element.23.mine_ref, f32[288,128]{1,0:T(8,128)S(1)} %collective-permute-done.1.theirs_ref, ...), custom_call_target="tpu_custom_call" | custom-call | bytes 1048576 | tf_op jit(solution)/shard_map/scores/pallas_call | solution.py:321
  43.9 21.1 %all_to_all.21 = bf16[128,8,128]{2,1,0:T(8,128)(2,1)S(1)} all-to-all(bf16[128,8,128]{2,1,0:T(8,128)(2,1)S(1)} %bitcast.13), channel_id=1, replica_groups=mesh['dp'=128,'group'=2] {'dp'}, dimensions={0} | all-to-all | bytes 524288 | tf_op jit(solution)/shard_map/all_to_all | solution.py:272
  65.0 0.9 mixed_gradient.1
  65.9 0.1 collective-permute-start.2
  66.0 1.3 %weight_gradient_own_half.1 = (f32[768,768]{1,0:T(8,128)S(1)}, f32[256,768]{1,0:T(8,128)S(1)}) custom-call(s32[2]{0:T(128)S(1)} %pad_add_fusion.place, bf16[256,768]{1,0:T(8,128)(2,1)S(1)} %get-tuple-element.28.mine_ref, bf16[256,768]{1,0:T(8,128)(2,1)S(1)} %convolution.1.hidden_ref, bf16[1536,768]{1,0:T(8,128)(2,1)S(1)} %copy-done.1), custom_call_target="tpu_custom_call" | custom-call | flops 603979776 | bytes 1048576 | tf_op jit(solution)/shard_map/weight_gradient_own_half/pallas_call | solution.py:343
  67.3 0.4 collective-permute-done.2.theirs_ref
  67.7 2.0 %weight_gradient.1 = bf16[16,104,768]{2,1,0:T(8,128)(2,1)S(1)} custom-call(s32[2]{0:T(128)S(1)} %pad_add_fusion.place, bf16[256,768]{1,0:T(8,128)(2,1)S(1)} %collective-permute-done.2.theirs_ref, bf16[256,768]{1,0:T(8,128)(2,1)S(1)} %convolution.1.hidden_ref, bf16[1536,768]{1,0:T(8,128)(2,1)S(1)} %copy-done.1, bf16[256,768]{1,0:T(8,128)(2,1)S(1)} %bitcast.10, ...), custom_call_target="tpu_custom_call" | custom-call | flops 603979776 | bytes 1048576 | tf_op jit(solution)/shard_map/weight_gradient/pallas_call | solution.py:351
  69.7 37.6 %all_to_all.22.recv_ref = bf16[16,104,768]{2,1,0:T(8,128)(2,1)S(1)} all-to-all(bf16[16,104,768]{2,1,0:T(8,128)(2,1)S(1)} %weight_gradient.1), channel_id=1, replica_groups={{0,16,32,48,64,80,96,112,128,144,160,176,192,208,224,240},{2,18,34,50,6..., dimensions={0} | all-to-all | bytes 5111808 | tf_op jit(solution)/shard_map/all_to_all | solution.py:272
  107.3 0.3 sum_over_plane.1
  107.7 13.0 %all_to_all.23.recv_ref = bf16[8,120,128]{2,1,0:T(8,128)(2,1)S(1)} all-to-all(bf16[8,120,128]{2,1,0:T(8,128)(2,1)S(1)} %sum_over_plane.1), channel_id=1, replica_groups={{0,2,4,6,8,10,12,14},{16,18,20,22,24,26,28,30},{32,34,36,38,40,42,44,46..., dimensions={0} | all-to-all | bytes 491520 | tf_op jit(solution)/shard_map/all_to_all | solution.py:272
  120.7 1.2 %outputs.1 = (f32[128,768]{1,0:T(8,128)}, f32[7,768]{1,0:T(8,128)}, f32[12,768]{1,0:T(8,128)}) custom-call(bf16[8,120,128]{2,1,0:T(8,128)(2,1)S(1)} %all_to_all.23.recv_ref, f32[128,128]{1,0:T(8,128)S(1)} %get-tuple-element.32.coef_ref, f32[128,128]{1,0:T(8,128)S(1)} %get-tuple-element.33.kcoef_ref, f32[128,768]{1,0:T(8,128)S(1)} %get-tuple-element.34.first_ref, ...), custom_call_target="tpu_custom_call" | custom-call | bytes 1048576 | tf_op jit(solution)/shard_map/outputs/pallas_call | solution.py:370
  (17 shorter events, 0.1 us)
Async XLA Ops:
  0.6 6.5 %copy-start.8 = (s32[128,1]{0,1:T(1,128)S(1)}, s32[128,1]{0,1:T(1,128)}, u32[]{:S(2)}) copy-start(s32[128,1]{0,1:T(1,128)} %param.12) | copy-start | bytes 1540
  0.6 6.6 %copy-start.7 = (s32[128]{0:T(128)S(1)}, s32[128]{0:T(128)}, u32[]{:S(2)}) copy-start(s32[128]{0:T(128)} %param.13) | copy-start | bytes 1540
  0.7 1.0 copy-start.2
  1.7 0.7 copy-start.5
  3.5 1.7 %copy-start = (bf16[1536,768]{1,0:T(8,128)(2,1)S(1)}, bf16[1536,768]{1,0:T(8,128)(2,1)}, u32[]{:S(2)}) copy-start(bf16[1536,768]{1,0:T(8,128)(2,1)} %w_ref.7) | copy-start | bytes 7077892
  5.2 2.1 %copy-start.1 = (bf16[1536,768]{1,0:T(8,128)(2,1)S(1)}, bf16[1536,768]{1,0:T(8,128)(2,1)}, u32[]{:S(2)}) copy-start(bf16[1536,768]{1,0:T(8,128)(2,1)} %w_ref.7) | copy-start | bytes 7077892
  5.2 4.6 %copy-start.3 = (bf16[1,256,768]{2,1,0:T(8,128)(2,1)S(1)}, bf16[1,256,768]{2,1,0:T(8,128)(2,1)}, u32[]{:S(2)}) copy-start(bf16[1,256,768]{2,1,0:T(8,128)(2,1)} %param.7) | copy-start | bytes 1179652
  7.1 2.6 %collective-permute-start = (f32[256,768]{1,0:T(8,128)}, f32[256,768]{1,0:T(8,128)}, u32[]{:S(2)}, u32[]{:S(2)}) collective-permute-start(f32[256,768]{1,0:T(8,128)} %other_half.1), channel_id=1, source_target_pairs={{0,1},{1,0},{2,3},{3,2},{4,5},{5,4},{6,7},{7,6},{8,9},{9,8},{10,11... | collective-permute-start | bytes 2359304 | tf_op jit(solution)/shard_map/ppermute | solution.py:296
  7.3 33.4 %copy-start.4 = (bf16[128,768]{1,0:T(8,128)(2,1)S(1)}, bf16[128,768]{1,0:T(8,128)(2,1)}, u32[]{:S(2)}) copy-start(bf16[128,768]{1,0:T(8,128)(2,1)} %bank_ref.5) | copy-start | bytes 589828
  7.3 33.4 %copy-start.6 = (bf16[1,768]{1,0:T(2,128)(2,1)S(1)}, bf16[1,768]{1,0:T(2,128)(2,1)}, u32[]{:S(2)}) copy-start(bf16[1,768]{1,0:T(2,128)(2,1)} %pos_ref.3) | copy-start | bytes 4612
  41.2 1.4 %collective-permute-start.1 = (f32[288,128]{1,0:T(8,128)S(1)}, f32[288,128]{1,0:T(8,128)S(1)}, u32[]{:S(2)}, u32[]{:S(2)}) collective-permute-start(f32[288,128]{1,0:T(8,128)S(1)} %get-tuple-element.23.mine_ref), channel_id=1, source_target_pairs={{0,1},{1,0},{2,3},{3,2},{4,5},{5,4},{6,7},{7,6},{8,9},{9,8},{10,11... | collective-permute-start | bytes 442376 | tf_op jit(solution)/shard_map/ppermute | solution.py:320
  65.9 1.8 %collective-permute-start.2 = (bf16[256,768]{1,0:T(8,128)(2,1)S(1)}, bf16[256,768]{1,0:T(8,128)(2,1)S(1)}, u32[]{:S(2)}, u32[]{:S(2)}) collective-permute-start(bf16[256,768]{1,0:T(8,128)(2,1)S(1)} %get-tuple-element.28.mine_ref), channel_id=1, source_target_pairs={{0,1},{1,0},{2,3},{3,2},{4,5},{5,4},{6,7},{7,6},{8,9},{9,8},{10,11... | collective-permute-start | bytes 1179656 | tf_op jit(solution)/shard_map/ppermute | solution.py:342

commit v4 on v3

--- a/solution.py
+++ b/solution.py
@@ -44,16 +44,16 @@
     return lax.dot_general(a, b, dims, precision=precision, preferred_element_type=F32)
 
 
-def call(body, outs, name, scratch=(), scalars=0, n_in=0, flops=0, moved=1 << 20):
+def call(body, outs, name, scratch=(), scalars=0, n_in=0, flops=0, moved=1 << 20, in_hbm=0, limit=VMEM_BYTES):
     smem = [pl.BlockSpec(memory_space=pltpu.SMEM)] * scalars
     vmem = [pl.BlockSpec(memory_space=pltpu.VMEM)] * n_in
     return pl.pallas_call(
         body,
         out_shape=[jax.ShapeDtypeStruct(s, d) for s, d in outs],
-        in_specs=smem + vmem,
+        in_specs=smem + [pl.BlockSpec(memory_space=pl.ANY)] * in_hbm + vmem,
         out_specs=[pl.BlockSpec(memory_space=pltpu.VMEM)] * len(outs),
         scratch_shapes=list(scratch),
-        compiler_params=pltpu.CompilerParams(vmem_limit_bytes=VMEM_BYTES),
+        compiler_params=pltpu.CompilerParams(vmem_limit_bytes=limit),
         cost_estimate=pl.CostEstimate(flops=flops, bytes_accessed=moved, transcendentals=0),
         name=name,
     )
@@ -66,18 +66,18 @@
         pad[8 + t : 40 + t, :] = tokens_ref[t : t + 32, :].astype(F32)
 
 
-def conv_body(tokens_ref, dw_ref, hidden_ref, pad):
+def conv_body(place, w_hbm, tokens_ref, dw_ref, hidden_ref, other_ref, pad, w_ref, sem):
+    start = pl.multiple_of((1 - place[0]) * HALF, HALF)
+    copy = pltpu.make_async_copy(w_hbm.at[pl.ds(start, HALF), :], w_ref, sem)
+    copy.start()
     fill_padded(tokens_ref, pad)
     for t in range(0, LEN, 32):
         total = jnp.zeros((32, HALF), F32)
         for k in range(KW):
             total = total + dw_ref[k : k + 1, :] * pad[5 + k + t : 37 + k + t, :]
         hidden_ref[t : t + 32, :] = total.astype(BF16)
-
-
-def other_body(place, hidden_ref, w_ref, other_ref):
-    start = pl.multiple_of((1 - place[0]) * HALF, HALF)
-    other_ref[...] = dot(hidden_ref[...], w_ref[pl.ds(start, HALF), :], NT)
+    copy.wait()
+    other_ref[...] = dot(hidden_ref[...], w_ref[...], NT)
 
 
 def own_body(place, hidden_ref, w_ref, owner_ref, block_ref, own_ref, table_ref):
@@ -287,12 +287,17 @@
     stage = pltpu.VMEM((N_DP * SLOT, LANES), F32)
     flops = 2 * LEN * HALF * HALF
 
-    (hidden,) = call(conv_body, [((LEN, HALF), BF16)], "convolution", [pad], n_in=2, moved=16 << 20)(
-        tokens, dw_kernel
-    )
-    (other,) = call(
-        other_body, [((LEN, HALF), F32)], "other_half", scalars=1, n_in=2, flops=flops
-    )(place, hidden, point_weight)
+    hidden, other = call(
+        conv_body,
+        [((LEN, HALF), BF16), ((LEN, HALF), F32)],
+        "convolution_and_other_half",
+        [pad, pltpu.VMEM((HALF, HALF), BF16), pltpu.SemaphoreType.DMA],
+        scalars=1,
+        in_hbm=1,
+        n_in=2,
+        flops=flops,
+        limit=62 * 2**20,
+    )(place, point_weight, tokens, dw_kernel)
     theirs = lax.ppermute(other, "group", SWAP)
     own, table = call(
         own_body,

time: 122 us -> 121 us (level)
  waiting for transfers between devices: 3.14 us -> 1.72 us
    ppermute x1, waiting for transfers between devices: 1.41 us -> 0.01 us  [per_device(): theirs = lax.ppermute(other, 'group', SWAP)]
    pallas_call x2 -> x1, Pallas kernels: 2.98 us -> 3.75 us  [per_device(): call(conv_body, [((LEN, HALF), BF16), ((LEN, HALF), F32)], 'convolution_a...]
    unnamed x19 -> x21, local copies, waits for them, and re-layouts: 3.53 us -> 2.8 us
  transfers between devices with their start and end apart: 3 -> 3, of which waited for: 3 -> 2; matrix products, arithmetic and copies ran while one was open for 0% -> 0% of each run, Pallas kernels for 2% -> 2%
where the time goes in v4:
time: 121 us; the launch traced here: 120 us
  blocking collectives  101 us (83%)
  Pallas kernels  13.3 us (11%)
  local copies, waits for them, and re-layouts  2.8 us (2%)
  waiting for transfers between devices  1.72 us (1%)
    all_to_all x4, blocking collectives, exchange(): lax.all_to_all(value, DP, split_axis=0, concat_axis=0, tiled=True, axis_i...  101 us
    pallas_call x1, Pallas kernels, per_device(): call(conv_body, [((LEN, HALF), BF16), ((LEN, HALF), F32)], 'convolution_a...  3.75 us
    unnamed x21, local copies, waits for them, and re-layouts  2.8 us
  transfers between devices with their start and end apart: 3, of which 2 were waited for; matrix products, arithmetic and copies ran while one was open for 0% of the time, Pallas kernels for 2%

profile of v4, /device:TPU:8, one launch (start us, length us, event | category | flops | bytes accessed | tf_op | source)
XLA Modules:
  0.0 120.4 jit_solution(16511184160527287777)
XLA Ops:
  0.7 0.6 pad_add_fusion.place
  1.2 3.8 %convolution_and_other_half.1 = (bf16[256,768]{1,0:T(8,128)(2,1)}, f32[256,768]{1,0:T(8,128)}) custom-call(s32[2]{0:T(128)} %pad_add_fusion.place, bf16[1536,768]{1,0:T(8,128)(2,1)} %w_ref.5, bf16[256,768]{1,0:T(8,128)(2,1)} %bitcast.8, f32[7,768]{1,0:T(8,128)} %dw_ref.1), custom_call_target="tpu_custom_call" | custom-call | flops 301989888 | bytes 1048576 | tf_op jit(solution)/shard_map/convolution_and_other_half/pallas_call | solution.py:290
  5.0 0.1 collective-permute-start
  5.1 0.1 copy.10.owner_ref
  5.2 0.0 copy-start
  5.2 1.7 %copy-done = bf16[1536,768]{1,0:T(8,128)(2,1)S(1)} copy-done((bf16[1536,768]{1,0:T(8,128)(2,1)S(1)}, bf16[1536,768]{1,0:T(8,128)(2,1)}, u32[]{:S(2)}) %copy-start) | copy-done | bytes 2359320
  6.9 1.0 copy-done.3
  7.9 1.1 own_half_and_requests.1
  9.0 0.8 embedding.1
  9.8 29.2 %all_to_all.20 = bf16[128,8,128]{2,1,0:T(8,128)(2,1)S(1)} all-to-all(bf16[128,8,128]{2,1,0:T(8,128)(2,1)S(1)} %bitcast.14), channel_id=1, replica_groups=mesh['dp'=128,'group'=2] {'dp'}, dimensions={0} | all-to-all | bytes 524288 | tf_op jit(solution)/shard_map/all_to_all | solution.py:272
  39.0 0.6 inner_products.1
  39.5 0.1 collective-permute-start.1
  39.6 1.4 %collective-permute-done.1.theirs_ref = f32[288,128]{1,0:T(8,128)S(1)} collective-permute-done((f32[288,128]{1,0:T(8,128)S(1)}, f32[288,128]{1,0:T(8,128)S(1)}, u32[]{:S(2)}, u32[]{:S(2)}) %collective-permute-start.1) | collective-permute-done | bytes 147488 | tf_op jit(solution)/shard_map/ppermute | solution.py:325
  41.0 1.3 %scores.1 = (bf16[1024,128]{1,0:T(8,128)(2,1)S(1)}, f32[128,128]{1,0:T(8,128)S(1)}, f32[128,128]{1,0:T(8,128)S(1)}, f32[24,128]{1,0:T(8,128)S(1)}) custom-call(s32[2]{0:T(128)S(1)} %copy-done.6, f32[288,128]{1,0:T(8,128)S(1)} %get-tuple-element.27.mine_ref, f32[288,128]{1,0:T(8,128)S(1)} %collective-permute-done.1.theirs_ref, ...), custom_call_target="tpu_custom_call" | custom-call | bytes 1048576 | tf_op jit(solution)/shard_map/scores/pallas_call | solution.py:326
  42.3 21.2 %all_to_all.21 = bf16[128,8,128]{2,1,0:T(8,128)(2,1)S(1)} all-to-all(bf16[128,8,128]{2,1,0:T(8,128)(2,1)S(1)} %bitcast.13), channel_id=1, replica_groups=mesh['dp'=128,'group'=2] {'dp'}, dimensions={0} | all-to-all | bytes 524288 | tf_op jit(solution)/shard_map/all_to_all | solution.py:272
  63.5 0.9 mixed_gradient.1
  64.3 0.1 collective-permute-start.2
  64.5 1.3 %weight_gradient_own_half.1 = (f32[768,768]{1,0:T(8,128)S(1)}, f32[256,768]{1,0:T(8,128)S(1)}) custom-call(s32[2]{0:T(128)S(1)} %copy-done.6, bf16[256,768]{1,0:T(8,128)(2,1)S(1)} %get-tuple-element.32.mine_ref, bf16[256,768]{1,0:T(8,128)(2,1)S(1)} %copy-done.4, bf16[1536,768]{1,0:T(8,128)(2,1)S(1)} %copy-done.1), custom_call_target="tpu_custom_call" | custom-call | flops 603979776 | bytes 1048576 | tf_op jit(solution)/shard_map/weight_gradient_own_half/pallas_call | solution.py:348
  65.8 0.4 collective-permute-done.2.theirs_ref
  66.2 2.0 %weight_gradient.1 = bf16[16,104,768]{2,1,0:T(8,128)(2,1)S(1)} custom-call(s32[2]{0:T(128)S(1)} %copy-done.6, bf16[256,768]{1,0:T(8,128)(2,1)S(1)} %collective-permute-done.2.theirs_ref, bf16[256,768]{1,0:T(8,128)(2,1)S(1)} %copy-done.4, bf16[1536,768]{1,0:T(8,128)(2,1)S(1)} %copy-done.1, bf16[256,768]{1,0:T(8,128)(2,1)S(1)} %bitcast.10, ...), custom_call_target="tpu_custom_call" | custom-call | flops 603979776 | bytes 1048576 | tf_op jit(solution)/shard_map/weight_gradient/pallas_call | solution.py:356
  68.2 37.6 %all_to_all.22.recv_ref = bf16[16,104,768]{2,1,0:T(8,128)(2,1)S(1)} all-to-all(bf16[16,104,768]{2,1,0:T(8,128)(2,1)S(1)} %weight_gradient.1), channel_id=1, replica_groups={{0,16,32,48,64,80,96,112,128,144,160,176,192,208,224,240},{2,18,34,50,6..., dimensions={0} | all-to-all | bytes 5111808 | tf_op jit(solution)/shard_map/all_to_all | solution.py:272
  105.8 0.3 sum_over_plane.1
  106.2 13.0 %all_to_all.23.recv_ref = bf16[8,120,128]{2,1,0:T(8,128)(2,1)S(1)} all-to-all(bf16[8,120,128]{2,1,0:T(8,128)(2,1)S(1)} %sum_over_plane.1), channel_id=1, replica_groups={{0,2,4,6,8,10,12,14},{16,18,20,22,24,26,28,30},{32,34,36,38,40,42,44,46..., dimensions={0} | all-to-all | bytes 491520 | tf_op jit(solution)/shard_map/all_to_all | solution.py:272
  119.2 1.2 %outputs.1 = (f32[128,768]{1,0:T(8,128)}, f32[7,768]{1,0:T(8,128)}, f32[12,768]{1,0:T(8,128)}) custom-call(bf16[8,120,128]{2,1,0:T(8,128)(2,1)S(1)} %all_to_all.23.recv_ref, f32[128,128]{1,0:T(8,128)S(1)} %get-tuple-element.36.coef_ref, f32[128,128]{1,0:T(8,128)S(1)} %get-tuple-element.37.kcoef_ref, f32[128,768]{1,0:T(8,128)S(1)} %get-tuple-element.38.first_ref, ...), custom_call_target="tpu_custom_call" | custom-call | bytes 1048576 | tf_op jit(solution)/shard_map/outputs/pallas_call | solution.py:375
  (18 shorter events, 0.0 us)
Async XLA Ops:
  0.6 4.4 %copy-start.9 = (s32[128,1]{0,1:T(1,128)S(1)}, s32[128,1]{0,1:T(1,128)}, u32[]{:S(2)}) copy-start(s32[128,1]{0,1:T(1,128)} %param.12) | copy-start | bytes 1540
  0.6 4.6 %copy-start.8 = (s32[128]{0:T(128)S(1)}, s32[128]{0:T(128)}, u32[]{:S(2)}) copy-start(s32[128]{0:T(128)} %param.13) | copy-start | bytes 1540
  1.2 4.0 %copy-start.6 = (s32[2]{0:T(128)S(1)}, s32[2]{0:T(128)}, u32[]{:S(2)}) copy-start(s32[2]{0:T(128)} %pad_add_fusion.place) | copy-start | bytes 28
  1.2 7.7 %copy-start.2 = (bf16[1,256,768]{2,1,0:T(8,128)(2,1)S(1)}, bf16[1,256,768]{2,1,0:T(8,128)(2,1)}, u32[]{:S(2)}) copy-start(bf16[1,256,768]{2,1,0:T(8,128)(2,1)} %param.7) | copy-start | bytes 1179652
  5.0 4.0 %collective-permute-start = (f32[256,768]{1,0:T(8,128)}, f32[256,768]{1,0:T(8,128)S(1)}, u32[]{:S(2)}, u32[]{:S(2)}) collective-permute-start(f32[256,768]{1,0:T(8,128)} %get-tuple-element.23), channel_id=1, source_target_pairs={{0,1},{1,0},{2,3},{3,2},{4,5},{5,4},{6,7},{7,6},{8,9},{9,8},{10,11... | collective-permute-start | bytes 2359304 | tf_op jit(solution)/shard_map/ppermute | solution.py:301
  5.2 1.7 %copy-start = (bf16[1536,768]{1,0:T(8,128)(2,1)S(1)}, bf16[1536,768]{1,0:T(8,128)(2,1)}, u32[]{:S(2)}) copy-start(bf16[1536,768]{1,0:T(8,128)(2,1)} %w_ref.5) | copy-start | bytes 7077892
  6.9 1.0 copy-start.3
  7.9 31.1 %copy-start.5 = (bf16[128,768]{1,0:T(8,128)(2,1)S(1)}, bf16[128,768]{1,0:T(8,128)(2,1)}, u32[]{:S(2)}) copy-start(bf16[128,768]{1,0:T(8,128)(2,1)} %bank_ref.5) | copy-start | bytes 589828
  7.9 31.1 %copy-start.7 = (bf16[1,768]{1,0:T(2,128)(2,1)S(1)}, bf16[1,768]{1,0:T(2,128)(2,1)}, u32[]{:S(2)}) copy-start(bf16[1,768]{1,0:T(2,128)(2,1)} %pos_ref.3) | copy-start | bytes 4612
  9.0 55.5 %copy-start.1 = (bf16[1536,768]{1,0:T(8,128)(2,1)S(1)}, bf16[1536,768]{1,0:T(8,128)(2,1)}, u32[]{:S(2)}) copy-start(bf16[1536,768]{1,0:T(8,128)(2,1)} %w_ref.5) | copy-start | bytes 7077892
  9.0 55.5 %copy-start.4 = (bf16[256,768]{1,0:T(8,128)(2,1)S(1)}, bf16[256,768]{1,0:T(8,128)(2,1)}, u32[]{:S(2)}) copy-start(bf16[256,768]{1,0:T(8,128)(2,1)} %get-tuple-element.21.hidden_ref) | copy-start | bytes 1179652
  39.5 1.4 %collective-permute-start.1 = (f32[288,128]{1,0:T(8,128)S(1)}, f32[288,128]{1,0:T(8,128)S(1)}, u32[]{:S(2)}, u32[]{:S(2)}) collective-permute-start(f32[288,128]{1,0:T(8,128)S(1)} %get-tuple-element.27.mine_ref), channel_id=1, source_target_pairs={{0,1},{1,0},{2,3},{3,2},{4,5},{5,4},{6,7},{7,6},{8,9},{9,8},{10,11... | collective-permute-start | bytes 442376 | tf_op jit(solution)/shard_map/ppermute | solution.py:325
  64.3 1.8 %collective-permute-start.2 = (bf16[256,768]{1,0:T(8,128)(2,1)S(1)}, bf16[256,768]{1,0:T(8,128)(2,1)S(1)}, u32[]{:S(2)}, u32[]{:S(2)}) collective-permute-start(bf16[256,768]{1,0:T(8,128)(2,1)S(1)} %get-tuple-element.32.mine_ref), channel_id=1, source_target_pairs={{0,1},{1,0},{2,3},{3,2},{4,5},{5,4},{6,7},{7,6},{8,9},{9,8},{10,11... | collective-permute-start | bytes 1179656 | tf_op jit(solution)/shard_map/ppermute | solution.py:347

commit v5 on v4

--- a/solution.py
+++ b/solution.py
@@ -66,23 +66,28 @@
         pad[8 + t : 40 + t, :] = tokens_ref[t : t + 32, :].astype(F32)
 
 
-def conv_body(place, w_hbm, tokens_ref, dw_ref, hidden_ref, other_ref, pad, w_ref, sem):
-    start = pl.multiple_of((1 - place[0]) * HALF, HALF)
-    copy = pltpu.make_async_copy(w_hbm.at[pl.ds(start, HALF), :], w_ref, sem)
-    copy.start()
+def conv_body(
+    place, w_hbm, tokens_ref, dw_ref, hidden_ref, other_ref, own_ref, pad, w_ref, sems
+):
+    copies = []
+    for i, side in enumerate((1 - place[0], place[0])):
+        start = pl.multiple_of(side * HALF, HALF)
+        copies.append(
+            pltpu.make_async_copy(w_hbm.at[pl.ds(start, HALF), :], w_ref.at[i], sems.at[i])
+        )
+        copies[i].start()
     fill_padded(tokens_ref, pad)
     for t in range(0, LEN, 32):
         total = jnp.zeros((32, HALF), F32)
         for k in range(KW):
             total = total + dw_ref[k : k + 1, :] * pad[5 + k + t : 37 + k + t, :]
         hidden_ref[t : t + 32, :] = total.astype(BF16)
-    copy.wait()
-    other_ref[...] = dot(hidden_ref[...], w_ref[...], NT)
-
-
-def own_body(place, hidden_ref, w_ref, owner_ref, block_ref, own_ref, table_ref):
-    start = pl.multiple_of(place[0] * HALF, HALF)
-    own_ref[...] = dot(hidden_ref[...], w_ref[pl.ds(start, HALF), :], NT)
+    for i, out in enumerate((other_ref, own_ref)):
+        copies[i].wait()
+        out[...] = dot(hidden_ref[...], w_ref[i], NT)
+
+
+def table_body(owner_ref, block_ref, table_ref):
     lane = lax.broadcasted_iota(jnp.int32, (OWN, LANES), 1)
     named = (owner_ref[...] == lane).astype(F32)
     blocks = jnp.broadcast_to(block_ref[...].astype(F32), (LANES, OWN)).T
@@ -287,11 +292,11 @@
     stage = pltpu.VMEM((N_DP * SLOT, LANES), F32)
     flops = 2 * LEN * HALF * HALF
 
-    hidden, other = call(
+    hidden, other, own = call(
         conv_body,
-        [((LEN, HALF), BF16), ((LEN, HALF), F32)],
-        "convolution_and_other_half",
-        [pad, pltpu.VMEM((HALF, HALF), BF16), pltpu.SemaphoreType.DMA],
+        [((LEN, HALF), BF16), ((LEN, HALF), F32), ((LEN, HALF), F32)],
+        "convolution_and_product",
+        [pad, pltpu.VMEM((2, HALF, HALF), BF16), pltpu.SemaphoreType.DMA((2,))],
         scalars=1,
         in_hbm=1,
         n_in=2,
@@ -299,14 +304,9 @@
         limit=62 * 2**20,
     )(place, point_weight, tokens, dw_kernel)
     theirs = lax.ppermute(other, "group", SWAP)
-    own, table = call(
-        own_body,
-        [((LEN, HALF), F32), ((N_DP, LANES), F32)],
-        "own_half_and_requests",
-        scalars=1,
-        n_in=4,
-        flops=flops,
-    )(place, hidden, point_weight, neg_owner, neg_block.reshape(1, OWN))
+    (table,) = call(table_body, [((N_DP, LANES), F32)], "requests", n_in=2)(
+        neg_owner, neg_block.reshape(1, OWN)
+    )
     slope, emb, send = call(
         embed_body,
         [((LEN, HALF), F32), ((8, HALF), F32), ((N_DP * SLOT, LANES), BF16)],

time: 121 us -> 121 us (level)
  waiting for transfers between devices: 1.72 us -> 3.8 us
  local copies, waits for them, and re-layouts: 2.8 us -> 1.28 us
    ppermute x1, waiting for transfers between devices: 0.01 us -> 2.08 us  [per_device(): theirs = lax.ppermute(other, 'group', SWAP)]
    unnamed x21 -> x19, local copies, waits for them, and re-layouts: 2.8 us -> 1.28 us
  transfers between devices with their start and end apart: 3 -> 3, of which waited for: 2 -> 3; matrix products, arithmetic and copies ran while one was open for 0% -> 0% of each run, Pallas kernels for 2% -> 1%
where the time goes in v5:
time: 121 us
  blocking collectives  101 us (83%)
  Pallas kernels  13.2 us (11%)
  waiting for transfers between devices  3.8 us (3%)
  local copies, waits for them, and re-layouts  1.28 us (1%)
    all_to_all x4, blocking collectives, exchange(): lax.all_to_all(value, DP, split_axis=0, concat_axis=0, tiled=True, axis_i...  101 us
    pallas_call x1, Pallas kernels, per_device(): call(conv_body, [((LEN, HALF), BF16), ((LEN, HALF), F32), ((LEN, HALF), F...  4.46 us
  transfers between devices with their start and end apart: 3, of which 3 were waited for; matrix products, arithmetic and copies ran while one was open for 0% of the time, Pallas kernels for 1%

profile of v5, /device:TPU:8, one launch (start us, length us, event | category | flops | bytes accessed | tf_op | source)
XLA Modules:
  0.0 120.7 jit_solution(11447297323525478910)
XLA Ops:
  0.6 0.0 copy-start.1
  0.7 0.7 pad_add_fusion.place
  1.3 4.5 %convolution_and_product.1 = (bf16[256,768]{1,0:T(8,128)(2,1)}, f32[256,768]{1,0:T(8,128)}, f32[256,768]{1,0:T(8,128)}) custom-call(s32[2]{0:T(128)} %pad_add_fusion.place, bf16[1536,768]{1,0:T(8,128)(2,1)} %w_ref.3, bf16[256,768]{1,0:T(8,128)(2,1)} %bitcast.8, f32[7,768]{1,0:T(8,128)} %dw_ref.1), custom_call_target="tpu_custom_call" | custom-call | flops 301989888 | bytes 1048576 | tf_op jit(solution)/shard_map/convolution_and_product/pallas_call | solution.py:295
  5.8 0.1 collective-permute-start
  5.9 0.1 copy.10.owner_ref
  6.0 0.3 requests.1.table_ref
  6.3 2.1 %collective-permute-done.other_ref = f32[256,768]{1,0:T(8,128)S(1)} collective-permute-done((f32[256,768]{1,0:T(8,128)}, f32[256,768]{1,0:T(8,128)S(1)}, u32[]{:S(2)}, u32[]{:S(2)}) %collective-permute-start) | collective-permute-done | bytes 786464 | tf_op jit(solution)/shard_map/ppermute | solution.py:306
  8.4 1.1 copy-done.4
  9.5 0.8 embedding.1
  10.3 29.1 %all_to_all.20 = bf16[128,8,128]{2,1,0:T(8,128)(2,1)S(1)} all-to-all(bf16[128,8,128]{2,1,0:T(8,128)(2,1)S(1)} %bitcast.14), channel_id=1, replica_groups=mesh['dp'=128,'group'=2] {'dp'}, dimensions={0} | all-to-all | bytes 524288 | tf_op jit(solution)/shard_map/all_to_all | solution.py:277
  39.4 0.6 inner_products.1
  40.0 0.1 collective-permute-start.1
  40.0 1.4 %collective-permute-done.1.theirs_ref = f32[288,128]{1,0:T(8,128)S(1)} collective-permute-done((f32[288,128]{1,0:T(8,128)S(1)}, f32[288,128]{1,0:T(8,128)S(1)}, u32[]{:S(2)}, u32[]{:S(2)}) %collective-permute-start.1) | collective-permute-done | bytes 147488 | tf_op jit(solution)/shard_map/ppermute | solution.py:325
  41.4 1.3 %scores.1 = (bf16[1024,128]{1,0:T(8,128)(2,1)S(1)}, f32[128,128]{1,0:T(8,128)S(1)}, f32[128,128]{1,0:T(8,128)S(1)}, f32[24,128]{1,0:T(8,128)S(1)}) custom-call(s32[2]{0:T(128)S(1)} %copy-done.5, f32[288,128]{1,0:T(8,128)S(1)} %get-tuple-element.24.mine_ref, f32[288,128]{1,0:T(8,128)S(1)} %collective-permute-done.1.theirs_ref, ...), custom_call_target="tpu_custom_call" | custom-call | bytes 1048576 | tf_op jit(solution)/shard_map/scores/pallas_call | solution.py:326
  42.7 21.0 %all_to_all.21 = bf16[128,8,128]{2,1,0:T(8,128)(2,1)S(1)} all-to-all(bf16[128,8,128]{2,1,0:T(8,128)(2,1)S(1)} %bitcast.13), channel_id=1, replica_groups=mesh['dp'=128,'group'=2] {'dp'}, dimensions={0} | all-to-all | bytes 524288 | tf_op jit(solution)/shard_map/all_to_all | solution.py:277
  63.7 0.9 mixed_gradient.1
  64.6 0.1 collective-permute-start.2
  64.7 1.3 %weight_gradient_own_half.1 = (f32[768,768]{1,0:T(8,128)S(1)}, f32[256,768]{1,0:T(8,128)S(1)}) custom-call(s32[2]{0:T(128)S(1)} %copy-done.5, bf16[256,768]{1,0:T(8,128)(2,1)S(1)} %get-tuple-element.29.mine_ref, bf16[256,768]{1,0:T(8,128)(2,1)S(1)} %copy-done.3, bf16[1536,768]{1,0:T(8,128)(2,1)S(1)} %copy-done), custom_call_target="tpu_custom_call" | custom-call | flops 603979776 | bytes 1048576 | tf_op jit(solution)/shard_map/weight_gradient_own_half/pallas_call | solution.py:348
  66.1 0.4 collective-permute-done.2.theirs_ref
  66.4 2.0 %weight_gradient.1 = bf16[16,104,768]{2,1,0:T(8,128)(2,1)S(1)} custom-call(s32[2]{0:T(128)S(1)} %copy-done.5, bf16[256,768]{1,0:T(8,128)(2,1)S(1)} %collective-permute-done.2.theirs_ref, bf16[256,768]{1,0:T(8,128)(2,1)S(1)} %copy-done.3, bf16[1536,768]{1,0:T(8,128)(2,1)S(1)} %copy-done, bf16[256,768]{1,0:T(8,128)(2,1)S(1)} %bitcast.10, ...), custom_call_target="tpu_custom_call" | custom-call | flops 603979776 | bytes 1048576 | tf_op jit(solution)/shard_map/weight_gradient/pallas_call | solution.py:356
  68.5 37.6 %all_to_all.22.recv_ref = bf16[16,104,768]{2,1,0:T(8,128)(2,1)S(1)} all-to-all(bf16[16,104,768]{2,1,0:T(8,128)(2,1)S(1)} %weight_gradient.1), channel_id=1, replica_groups={{0,16,32,48,64,80,96,112,128,144,160,176,192,208,224,240},{2,18,34,50,6..., dimensions={0} | all-to-all | bytes 5111808 | tf_op jit(solution)/shard_map/all_to_all | solution.py:277
  106.1 0.3 sum_over_plane.1
  106.5 13.0 %all_to_all.23.recv_ref = bf16[8,120,128]{2,1,0:T(8,128)(2,1)S(1)} all-to-all(bf16[8,120,128]{2,1,0:T(8,128)(2,1)S(1)} %sum_over_plane.1), channel_id=1, replica_groups={{0,2,4,6,8,10,12,14},{16,18,20,22,24,26,28,30},{32,34,36,38,40,42,44,46..., dimensions={0} | all-to-all | bytes 491520 | tf_op jit(solution)/shard_map/all_to_all | solution.py:277
  119.5 1.2 %outputs.1 = (f32[128,768]{1,0:T(8,128)}, f32[7,768]{1,0:T(8,128)}, f32[12,768]{1,0:T(8,128)}) custom-call(bf16[8,120,128]{2,1,0:T(8,128)(2,1)S(1)} %all_to_all.23.recv_ref, f32[128,128]{1,0:T(8,128)S(1)} %get-tuple-element.34.coef_ref, f32[128,128]{1,0:T(8,128)S(1)} %get-tuple-element.35.kcoef_ref, f32[128,768]{1,0:T(8,128)S(1)} %get-tuple-element.36.first_ref, ...), custom_call_target="tpu_custom_call" | custom-call | bytes 1048576 | tf_op jit(solution)/shard_map/outputs/pallas_call | solution.py:375
  (16 shorter events, 0.0 us)
Async XLA Ops:
  0.6 7.8 %copy-start.1 = (bf16[1,256,768]{2,1,0:T(8,128)(2,1)S(1)}, bf16[1,256,768]{2,1,0:T(8,128)(2,1)}, u32[]{:S(2)}) copy-start(bf16[1,256,768]{2,1,0:T(8,128)(2,1)} %param.7) | copy-start | bytes 1179652
  0.6 5.3 %copy-start.8 = (s32[128,1]{0,1:T(1,128)S(1)}, s32[128,1]{0,1:T(1,128)}, u32[]{:S(2)}) copy-start(s32[128,1]{0,1:T(1,128)} %param.12) | copy-start | bytes 1540
  0.7 5.4 %copy-start.7 = (s32[128]{0:T(128)S(1)}, s32[128]{0:T(128)}, u32[]{:S(2)}) copy-start(s32[128]{0:T(128)} %param.13) | copy-start | bytes 1540
  1.3 38.1 %copy-start.2 = (bf16[128,768]{1,0:T(8,128)(2,1)S(1)}, bf16[128,768]{1,0:T(8,128)(2,1)}, u32[]{:S(2)}) copy-start(bf16[128,768]{1,0:T(8,128)(2,1)} %bank_ref.5) | copy-start | bytes 589828
  1.3 38.1 %copy-start.6 = (bf16[1,768]{1,0:T(2,128)(2,1)S(1)}, bf16[1,768]{1,0:T(2,128)(2,1)}, u32[]{:S(2)}) copy-start(bf16[1,768]{1,0:T(2,128)(2,1)} %pos_ref.3) | copy-start | bytes 4612
  1.3 40.0 %copy-start.5 = (s32[2]{0:T(128)S(1)}, s32[2]{0:T(128)}, u32[]{:S(2)}) copy-start(s32[2]{0:T(128)} %pad_add_fusion.place) | copy-start | bytes 28
  5.8 2.6 %collective-permute-start = (f32[256,768]{1,0:T(8,128)}, f32[256,768]{1,0:T(8,128)S(1)}, u32[]{:S(2)}, u32[]{:S(2)}) collective-permute-start(f32[256,768]{1,0:T(8,128)} %get-tuple-element.21), channel_id=1, source_target_pairs={{0,1},{1,0},{2,3},{3,2},{4,5},{5,4},{6,7},{7,6},{8,9},{9,8},{10,11... | collective-permute-start | bytes 2359304 | tf_op jit(solution)/shard_map/ppermute | solution.py:306
  8.4 1.1 copy-start.4
  9.5 55.2 %copy-start = (bf16[1536,768]{1,0:T(8,128)(2,1)S(1)}, bf16[1536,768]{1,0:T(8,128)(2,1)}, u32[]{:S(2)}) copy-start(bf16[1536,768]{1,0:T(8,128)(2,1)} %w_ref.3) | copy-start | bytes 7077892
  9.5 55.2 %copy-start.3 = (bf16[256,768]{1,0:T(8,128)(2,1)S(1)}, bf16[256,768]{1,0:T(8,128)(2,1)}, u32[]{:S(2)}) copy-start(bf16[256,768]{1,0:T(8,128)(2,1)} %get-tuple-element.30.hidden_ref) | copy-start | bytes 1179652
  40.0 1.4 %collective-permute-start.1 = (f32[288,128]{1,0:T(8,128)S(1)}, f32[288,128]{1,0:T(8,128)S(1)}, u32[]{:S(2)}, u32[]{:S(2)}) collective-permute-start(f32[288,128]{1,0:T(8,128)S(1)} %get-tuple-element.24.mine_ref), channel_id=1, source_target_pairs={{0,1},{1,0},{2,3},{3,2},{4,5},{5,4},{6,7},{7,6},{8,9},{9,8},{10,11... | collective-permute-start | bytes 442376 | tf_op jit(solution)/shard_map/ppermute | solution.py:325
  64.6 1.8 %collective-permute-start.2 = (bf16[256,768]{1,0:T(8,128)(2,1)S(1)}, bf16[256,768]{1,0:T(8,128)(2,1)S(1)}, u32[]{:S(2)}, u32[]{:S(2)}) collective-permute-start(bf16[256,768]{1,0:T(8,128)(2,1)S(1)} %get-tuple-element.29.mine_ref), channel_id=1, source_target_pairs={{0,1},{1,0},{2,3},{3,2},{4,5},{5,4},{6,7},{7,6},{8,9},{9,8},{10,11... | collective-permute-start | bytes 1179656 | tf_op jit(solution)/shard_map/ppermute | solution.py:347
